TPU v7x, 32 devices: a whole 2x2x4 slice. The times are simulated.
32 devices in a mesh: wall: 2 (over x), plane: 16 (over z, y, core).
Axes of the slice: x: 2, y: 2, z: 4, core: 2. Of those that a mesh axis runs over, the one named last changes fastest.
Arguments:
- jacobian: float32 [3, 16, 16, 32, 16, 128], P(None, None, None, 'wall', 'plane'), as said below
- residual: float32 [16, 32, 16, 128], P(None, 'wall', 'plane')
- previous_update: float32 [16, 32, 16, 128], P(None, 'wall', 'plane'), may hold values from -6 to 6
- offline_coupling: float32 [4, 16, 32, 16, 128], P(None, None, 'wall', 'plane'), may hold values from 0.003 to 0.03
- wake_partner: int32 [16, 128], P('plane'), may hold values from 0 to 127, each once within a row
- line_length: int32 [16, 128], P('plane'), may hold values from 16 to 32
- bottom_flag: int32 [16, 128], P('plane'), may hold values 0 or 1
Outputs:
- update: float32 [16, 32, 16, 128], P(None, 'wall', 'plane')
Inputs may be any that keep to these rules, and one draw needn't show every extreme that they name: jacobian[2, :, :, k] is the transpose of jacobian[0, :, :, k + 1], every jacobian[1, :, :, k] is symmetric, and every row of a line's matrix is strictly diagonally dominant with a positive diagonal. `bottom_flag`: 1 where a column's first cell lies on the wake cut, 0 where it lies on the capsule wall. `wake_partner`: for a wake-cut column (i, j), the spanwise index of the column at station (i + 8) modulo 16, on the other branch of the cut, that lies beneath its first cell; each row is a permutation of 0 to 127.
All inputs are finite; a program needn't handle non-finite values. No bound on the sum of `bottom_flag` on one device may be relied on, other than what follows from the above.
Results may differ from a plain program's by a relative error of at most 0.0003.
Values sent between devices are 32-bit elements; how exact they have to be, the bound alone decides.
A program may use at most 192 MiB of HBM per device.

v0:
```python
import jax
import jax.numpy as jnp
from jax import lax
from jax.sharding import PartitionSpec as P

precise = lax.Precision.HIGHEST


def with_halo(block, sides, width):
    for axis, dim in sides:
        count = lax.axis_size(axis)
        forward = [(i, i + 1) for i in range(count - 1)]
        backward = [(target, source) for source, target in forward]
        low = lax.ppermute(
            lax.slice_in_dim(block, block.shape[dim] - width, None, axis=dim), axis, forward
        )
        high = lax.ppermute(lax.slice_in_dim(block, 0, width, axis=dim), axis, backward)
        block = jnp.concatenate([low, block, high], axis=dim)
    return block


def from_behind(block, axis, distance):
    devices = range(lax.axis_size(axis))
    route = [(i - distance, i) for i in devices if i - distance in devices]
    return lax.ppermute(block, axis, route)


def product(left, right):
    return jnp.einsum("vwc,wuc->vuc", left, right, precision=precise)


def solve_block(matrix, given):
    extent = matrix.shape[0]
    augmented = jnp.concatenate([matrix, given], axis=1)
    for pivot in range(extent):
        pivot_row = augmented[pivot] / augmented[pivot, pivot][None, :]
        augmented = augmented - augmented[:, pivot][:, None, :] * pivot_row[None]
        augmented = augmented.at[pivot].set(pivot_row)
    return augmented[:, extent:]


def effective(lower, middle, upper, active_here, active_above, not_bottom):
    identity = jnp.eye(lower.shape[0], dtype=jnp.float32)[:, :, None, None]
    return (
        lower * (active_here * not_bottom)[None, None],
        middle * active_here[None, None] + identity * (1.0 - active_here)[None, None],
        upper * active_above[None, None],
    )


def eliminate(lower, middle, upper, source, block_in, vector_in, levels):
    extent = lower.shape[0]
    blocks = jnp.zeros(lower.shape, jnp.float32)
    vectors = jnp.zeros(source.shape, jnp.float32)

    def advance(level, state):
        block_prev, vector_prev, blocks, vectors = state
        below = lax.dynamic_index_in_dim(lower, level, 2, keepdims=False)
        centre = lax.dynamic_index_in_dim(middle, level, 2, keepdims=False)
        above = lax.dynamic_index_in_dim(upper, level, 2, keepdims=False)
        given = lax.dynamic_index_in_dim(source, level, 2, keepdims=False)
        schur = centre - product(below, block_prev)
        reduced = given - product(below, vector_prev)
        joined = solve_block(schur, jnp.concatenate([above, reduced], axis=1))
        block_next = joined[:, :extent]
        vector_next = joined[:, extent:]
        blocks = lax.dynamic_update_index_in_dim(blocks, block_next, level, 2)
        vectors = lax.dynamic_update_index_in_dim(vectors, vector_next, level, 2)
        return (block_next, vector_next, blocks, vectors)

    return lax.fori_loop(0, levels, advance, (block_in, vector_in, blocks, vectors))


def substitute(blocks, vectors, value_above, levels, result):

    def retreat(count, state):
        value_next, result = state
        level = levels - 1 - count
        block = lax.dynamic_index_in_dim(blocks, level, 2, keepdims=False)
        vector = lax.dynamic_index_in_dim(vectors, level, 2, keepdims=False)
        value = vector - product(block, value_next)
        result = lax.dynamic_update_index_in_dim(result, value, level, 2)
        return (value, result)

    return lax.fori_loop(0, levels, retreat, (value_above, result))


def per_device(
    jacobian, residual, previous_update, offline_coupling, wake_partner, line_length, bottom_flag
):
    unknowns = jacobian.shape[1]
    depth = jacobian.shape[3]
    stations = jacobian.shape[4]
    span = jacobian.shape[5]
    columns = stations * span
    wall_index = lax.axis_index("wall")
    plane_index = lax.axis_index("plane")
    planes = lax.axis_size("plane")
    padded = with_halo(previous_update, (("plane", 2),), 1)
    offline = (
        offline_coupling[0] * padded[:, :, :-2]
        + offline_coupling[1] * padded[:, :, 2:]
        + offline_coupling[2] * jnp.roll(previous_update, 1, axis=3)
        + offline_coupling[3] * jnp.roll(previous_update, -1, axis=3)
    )
    bottom_row = previous_update[:, 0]
    mirror_index = (plane_index + planes // 2) % planes
    whole = lax.all_gather(bottom_row, "plane", axis=1, tiled=True)
    facing = lax.dynamic_slice_in_dim(whole, mirror_index * stations, stations, 1)
    partner = jnp.take_along_axis(facing, wake_partner[None], axis=2)
    weight = bottom_flag.astype(jnp.float32) * (wall_index == 0).astype(jnp.float32)
    wake = (
        jnp.einsum("vwij,wij->vij", jacobian[0, :, :, 0], partner, precision=precise) * weight[None]
    )
    levels = wall_index * depth + jnp.arange(depth, dtype=jnp.int32)
    active = (levels[:, None, None] < line_length[None]).astype(jnp.float32)
    active_above = ((levels + 1)[:, None, None] < line_length[None]).astype(jnp.float32)
    not_bottom = (levels > 0).astype(jnp.float32)[:, None]
    source = residual + offline
    source = source.at[:, 0].add(-wake)
    source = (source * active[None]).reshape(unknowns, 1, depth, columns)
    blocks = jacobian.reshape(3, unknowns, unknowns, depth, columns)
    lower, middle, upper = effective(
        blocks[0],
        blocks[1],
        blocks[2],
        active.reshape(depth, columns),
        active_above.reshape(depth, columns),
        not_bottom,
    )
    empty_block = jnp.zeros((unknowns, unknowns, columns), jnp.float32)
    empty_vector = jnp.zeros((unknowns, 1, columns), jnp.float32)
    block_in = empty_block
    vector_in = empty_vector
    parts = eliminate(lower, middle, upper, source, block_in, vector_in, depth)
    handed = from_behind(
        jnp.concatenate([parts[2][:, :, depth - 1], parts[3][:, :, depth - 1]], axis=1), "wall", 1
    )
    block_in = handed[:, :unknowns]
    vector_in = handed[:, unknowns:]
    parts = eliminate(lower, middle, upper, source, block_in, vector_in, depth)
    value_above = empty_vector
    solved = substitute(
        parts[2], parts[3], value_above, depth, jnp.zeros(source.shape, jnp.float32)
    )
    value_above = from_behind(solved[1][:, :, 0], "wall", -1)
    solution = substitute(
        parts[2], parts[3], value_above, depth, jnp.zeros(source.shape, jnp.float32)
    )[1]
    return solution[:, 0].reshape(unknowns, depth, stations, span)


def solution(mesh):
    return jax.shard_map(
        per_device,
        mesh=mesh,
        in_specs=(
            P(None, None, None, "wall", "plane", None),
            P(None, "wall", "plane", None),
            P(None, "wall", "plane", None),
            P(None, None, "wall", "plane", None),
            P("plane", None),
            P("plane", None),
            P("plane", None),
        ),
        out_specs=P(None, "wall", "plane", None),
        check_vma=False,
    )
```

profile of v0, /device:TPU:0, one launch (start us, length us, event | category | flops | bytes accessed | tf_op | source)
XLA Modules:
  0.0 590.7 jit_solution(17977293387750040532)
XLA Ops:
  6.9 25.4 %all-gather = f32[16,16,1,128]{3,2,1,0:T(1,128)S(1)} all-gather(f32[16,1,1,128]{3,2,1,0:T(1,128)S(1)} %slice.2426), channel_id=2, replica_groups=mesh['wall'=2,'plane'=16] {'plane'}, dimensions={1}, use_global_device_ids=true | all-gather | bytes 139264 | tf_op jit(solution)/shard_map/all_gather | solution.py:108
  33.7 8.3 %fusion.22 = (f32[1,16,16,16,1,128]{5,4,3,2,1,0:T(1,128)}, f32[1,16,16,16,1,128]{5,4,3,2,1,0:T(1,128)}, f32[1,16,16,16,1,128]{5,4,3,2,1,0:T(1,128)S(1)}) fusion(f32[3,16,16,16,1,128]{5,4,3,2,1,0:T(1,128)} %param.81), kind=kLoop, calls=%fused_computation.232 | loop fusion | bytes 12582912 | tf_op jit(solution)/shard_map/slice | solution.py:126
  42.0 12.0 %copy.215 = f32[1,16,16,16,1,128]{2,1,5,3,4,0:T(8,128)} copy(f32[1,16,16,16,1,128]{5,4,3,2,1,0:T(1,128)} %get-tuple-element.1768) | data formatting | bytes 4194304
  54.0 10.7 %copy.216 = f32[1,16,16,16,1,128]{2,1,5,3,4,0:T(8,128)} copy(f32[1,16,16,16,1,128]{5,4,3,2,1,0:T(1,128)S(1)} %get-tuple-element.1769) | data formatting | bytes 4194304
  65.5 4.2 fusion.11
  69.6 13.8 %bitcast_multiply_fusion.2 = f32[16,16,16,128]{1,0,3,2:T(8,128)} fusion(f32[1,16,16,16,1,128]{2,1,5,3,4,0:T(8,128)} %copy.216, f32[16,128]{1,0:T(8,128)S(1)} %get-tuple-element.1778), kind=kLoop, calls=%fused_computation.189 | loop fusion | flops 524288 | bytes 4202496 | tf_op jit(solution)/shard_map/mul | solution.py:45
  86.1 6.7 %fusion.10 = f32[16,16,16,128]{1,0,3,2:T(8,128)} fusion(f32[1,16,16,16,1,128]{2,1,5,3,4,0:T(8,128)S(1)} %bitcast.632, f32[16,128]{1,0:T(8,128)S(1)} %get-tuple-element.1779, f32[16,16]{1,0:T(8,128)S(1)} %fusion.20, f32[16,128]{1,0:T(8,128)S(1)} %get-tuple-element.1781), kind=kLoop, calls=%fused_computation.191 | loop fusion | flops 1572864 | bytes 4211712 | tf_op jit(solution)/shard_map/add | solution.py:46
  95.1 185.2 %while.112 = (s32[]{:T(128)}, f32[16,16,128]{2,0,1:T(8,128)S(1)}, f32[16,1,128]{2,0,1:T(8,128)S(1)}, f32[16,16,16,128]{3,0,1,2:T(8,128)}, f32[16,1,16,128]{3,0,2...) while((s32[]{:T(128)}, f32[16,16,128]{2,0,1:T(8,128)S(1)}, ...), condition=%wide.region_1.2_spmd, body=%wide.region_0.1_spmd.sunk | while | flops 8890370 | bytes 15271725 | solution.py:71
  190.0 2.7 fusion.39
  281.3 3.6 collective-permute-start.2
  284.9 3.2 collective-permute-done.2
  288.1 249.3 %while.113 = (s32[]{:T(128)}, f32[16,16,128]{2,0,1:T(8,128)S(1)}, f32[16,1,128]{2,0,1:T(8,128)S(1)}, f32[16,16,16,128]{3,2,1,0:T(8,128)}, f32[16,1,16,128]{3,0,2...) while((s32[]{:T(128)}, f32[16,16,128]{2,0,1:T(8,128)S(1)}, ...), condition=%wide.region_3.4_spmd, body=%wide.region_2.3_spmd.sunk | while | flops 8890370 | bytes 15926577 | solution.py:71
  299.2 4.5 dynamic_update_slice.80
  314.8 4.5 dynamic_update_slice.80
  330.3 4.5 dynamic_update_slice.80
  345.9 4.5 dynamic_update_slice.80
  361.5 4.5 dynamic_update_slice.80
  377.0 4.5 dynamic_update_slice.80
  392.6 4.5 dynamic_update_slice.80
  408.2 4.5 dynamic_update_slice.80
  415.0 2.7 fusion.43
  423.8 4.5 dynamic_update_slice.80
  439.3 4.5 dynamic_update_slice.80
  454.9 4.5 dynamic_update_slice.80
  470.5 4.5 dynamic_update_slice.80
  486.1 4.5 dynamic_update_slice.80
  501.7 4.5 dynamic_update_slice.80
  517.3 4.5 dynamic_update_slice.80
  532.9 4.5 dynamic_update_slice.80
  537.4 23.7 %while.115 = (s32[]{:T(128)}, f32[16,1,128]{2,0,1:T(8,128)S(1)}, f32[16,1,16,128]{3,2,1,0:T(8,128)S(1)}, f32[16,1,16,128]{3,0,2,1:T(8,128)S(1)}, f32[16,16,16,12...) while((s32[]{:T(128)}, f32[16,1,128]{2,0,1:T(8,128)S(1)}, ...), condition=%wide.region_5.6_spmd.clone, body=%wide.region_4.5_spmd.clone.sunk | while | flops 67591 | bytes 467105 | solution.py:85
  562.4 4.2 collective-permute-done.3
  566.7 23.4 %while.114 = (s32[]{:T(128)}, f32[16,1,128]{2,0,1:T(8,128)S(1)}, f32[16,1,16,128]{3,2,1,0:T(8,128)S(1)}, f32[16,1,16,128]{3,0,2,1:T(8,128)S(1)}, f32[16,16,16,12...) while((s32[]{:T(128)}, f32[16,1,128]{2,0,1:T(8,128)S(1)}, ...), condition=%wide.region_7.8_spmd, body=%wide.region_6.7_spmd.sunk | while | flops 65542 | bytes 450711 | solution.py:85
  (3659 shorter events, 397.7 us)
Async XLA Ops:
  0.0 33.5 %copy-start.2 = (s32[1,128]{1,0:T(1,128)S(1)}, s32[1,128]{1,0:T(1,128)}, u32[]{:S(2)}) copy-start(s32[1,128]{1,0:T(1,128)} %param.86) | copy-start | bytes 1540
  1.0 92.9 %collective-permute-start = (f32[16,16,1,128]{3,0,1,2:T(8,128)S(1)}, f32[16,16,1,128]{3,0,1,2:T(8,128)S(1)}, u32[]{:S(2)}, u32[]{:S(2)}) collective-permute-start(f32[16,16,1,128]{3,0,1,2:T(8,128)S(1)} %copy.131), channel_id=1, source_target_pairs={{0,1},{1,2},{2,3},{3,4},{4,5},{5,6},{6,7},{7,8},{8,9},{9,10},{10,1... | collective-permute-start | bytes 393224 | tf_op jit(solution)/shard_map/ppermute | solution.py:14
  3.3 90.5 %collective-permute-start.1 = (f32[16,16,1,128]{3,0,1,2:T(8,128)S(1)}, f32[16,16,1,128]{3,0,1,2:T(8,128)}, u32[]{:S(2)}, u32[]{:S(2)}) collective-permute-start(f32[16,16,1,128]{3,0,1,2:T(8,128)S(1)} %copy.131), channel_id=1, source_target_pairs={{1,0},{2,1},{3,2},{4,3},{5,4},{6,5},{7,6},{8,7},{9,8},{10,9},{11,1... | collective-permute-start | bytes 393224 | tf_op jit(solution)/shard_map/ppermute | solution.py:17
  69.6 13.8 %slice-start = ((s8[16777216]{0:T(1024)(128)(4,1)}), s8[4194304]{0:T(1024)(128)(4,1)S(1)}, s32[]{:S(2)}) async-start(s8[16777216]{0:T(1024)(128)(4,1)} %bitcast.631), calls=%async_computation | async-start | bytes 8388608
  69.6 13.8 %slice-start.1 = ((s8[16777216]{0:T(1024)(128)(4,1)}), s8[4194304]{0:T(1024)(128)(4,1)S(1)}, s32[]{:S(2)}) async-start(s8[16777216]{0:T(1024)(128)(4,1)} %bitcast.631), calls=%async_computation.1 | async-start | bytes 8388608
  69.6 15.3 %slice-start.2 = ((s8[16777216]{0:T(1024)(128)(4,1)}), s8[4194304]{0:T(1024)(128)(4,1)S(1)}, s32[]{:S(2)}) async-start(s8[16777216]{0:T(1024)(128)(4,1)} %bitcast.631), calls=%async_computation.2 | async-start | bytes 8388608
  69.6 16.5 %slice-start.3 = ((s8[16777216]{0:T(1024)(128)(4,1)}), s8[4194304]{0:T(1024)(128)(4,1)S(1)}, s32[]{:S(2)}) async-start(s8[16777216]{0:T(1024)(128)(4,1)} %bitcast.631), calls=%async_computation.3 | async-start | bytes 8388608
  86.1 6.7 %copy-start.3 = (s32[1,128]{1,0:T(1,128)S(1)}, s32[1,128]{1,0:T(1,128)}, u32[]{:S(2)}) copy-start(s32[1,128]{1,0:T(1,128)} %param.87) | copy-start | bytes 1540
  86.1 7.7 %copy-start = (f32[16,16,1,128]{3,2,1,0:T(1,128)S(1)}, f32[16,16,1,128]{3,2,1,0:T(1,128)}, u32[]{:S(2)}) copy-start(f32[16,16,1,128]{3,2,1,0:T(1,128)} %param.82) | copy-start | bytes 393220
  281.3 6.8 %collective-permute-start.2 = (f32[16,17,128]{2,0,1:T(8,128)S(1)}, f32[16,17,128]{2,0,1:T(8,128)S(1)}, u32[]{:S(2)}, u32[]{:S(2)}) collective-permute-start(f32[16,17,128]{2,0,1:T(8,128)S(1)} %pad_maximum_fusion.2), channel_id=1, source_target_pairs={{0,16},{1,17},{2,18},{3,19},{4,20},{5,21},{6,22},{7,23},{8,24},{9,... | collective-permute-start | bytes 417800 | tf_op jit(solution)/shard_map/ppermute | solution.py:25
  561.1 5.5 collective-permute-start.3
  590.1 0.7 copy-start.1
where the time goes:
time: 597 us; the launch traced here: 591 us
  local copies, waits for them, and re-layouts  331 us (55%)
  other arithmetic  108 us (18%)
  matrix products  86.8 us (15%)
  blocking collectives  25.4 us (4%)
  loops' own time  23.4 us (4%)
  starting transfers between devices  8.53 us (1%)
  waiting for transfers between devices  7.46 us (1%)
    dot_general x32, matrix products, product(): return jnp.einsum('vwc,wuc->vuc', left, right, precision=precise)  86.8 us
    dynamic_update_slice x48, local copies, waits for them, and re-layouts, advance(): blocks = lax.dynamic_update_index_in_dim(blocks, block_next, level, 2)  84.8 us
    while x48, other arithmetic  50.4 us
    scatter x512, local copies, waits for them, and re-layouts, solve_block(): augmented = augmented.at[pivot].set(pivot_row)  44.3 us
    dynamic_slice x32, local copies, waits for them, and re-layouts, retreat(): block = lax.dynamic_index_in_dim(blocks, level, 2, keepdims=False)  42.4 us
    slice x32, local copies, waits for them, and re-layouts, solve_block(): pivot_row = augmented[pivot] / augmented[pivot, pivot][None, :]  32.9 us
    squeeze x32, local copies, waits for them, and re-layouts, advance(): above = lax.dynamic_index_in_dim(upper, level, 2, keepdims=False)  29.3 us
    unnamed x20, local copies, waits for them, and re-layouts  27.1 us
  transfers between devices with their start and end apart: 4, of which 2 were waited for; matrix products, arithmetic and copies ran while one was open for 10% of the time, Pallas kernels for 0%

commit v1 on v0

v1 whole, which is shorter than its diff:
```python
import functools

import jax
import jax.numpy as jnp
from jax import lax
from jax.experimental import pallas as pl
from jax.experimental.pallas import tpu as pltpu
from jax.sharding import PartitionSpec as P

MESH = pl.DeviceIdType.MESH


def spread(row, index, rows):
    return jnp.broadcast_to(row[index : index + 1, :], (rows, row.shape[1]))


def sweep(low, high, right):
    extent = len(low)
    half = low[0].shape[0]
    place = lax.broadcasted_iota(jnp.int32, low[0].shape, 0)
    for pivot in range(extent):
        in_low = pivot < half
        at = pivot % half
        pivot_low, pivot_high = low[pivot], high[pivot]
        inverse = 1.0 / spread(pivot_low if in_low else pivot_high, at, half)
        here = place == at
        scaled_low, scaled_high = pivot_low * inverse, pivot_high * inverse
        if in_low:
            scaled_low = jnp.where(here, -inverse, scaled_low)
        else:
            scaled_high = jnp.where(here, -inverse, scaled_high)
        if right is not None:
            scaled_right = tuple(part * inverse for part in right[pivot])
        order = [(pivot + 1 + step) % extent for step in range(extent - 1)]
        for row in order:
            factor = spread(pivot_low if row < half else pivot_high, row % half, half)
            kept_low, kept_high = low[row], high[row]
            if in_low:
                kept_low = jnp.where(here, 0.0, kept_low)
            else:
                kept_high = jnp.where(here, 0.0, kept_high)
            low[row] = kept_low - factor * scaled_low
            high[row] = kept_high - factor * scaled_high
            if right is not None:
                right[row] = tuple(
                    part - factor * scaled for part, scaled in zip(right[row], scaled_right)
                )
        low[pivot], high[pivot] = scaled_low, scaled_high
        if right is not None:
            right[pivot] = scaled_right


def total(terms):
    while len(terms) > 1:
        terms = [
            terms[at] + terms[at + 1] if at + 1 < len(terms) else terms[at]
            for at in range(0, len(terms), 2)
        ]
    return terms[0]


def kernel(
    extent,
    depth,
    jacobian,
    residual,
    previous,
    coupling,
    partner_map,
    length,
    flag,
    out,
    near,
    centre,
    first,
    schur,
    inverse,
    carry,
    masked,
    source,
    reduced,
    fixed,
    bottom,
    facing,
    from_left,
    from_right,
    block_out,
    block_in,
    vector_out,
    vector_in,
    copy_sems,
    send_sems,
    recv_sems,
):
    wall = lax.axis_index("wall")
    plane = lax.axis_index("plane")
    planes = lax.axis_size("plane")
    half = extent // 2
    right = {"wall": wall, "plane": lax.rem(plane + 1, planes)}
    left = {"wall": wall, "plane": lax.rem(plane + planes - 1, planes)}
    mirror = {"wall": wall, "plane": lax.rem(plane + planes // 2, planes)}
    across = {"wall": 1 - wall, "plane": plane}

    fetch_centre = pltpu.make_async_copy(jacobian.at[1], centre, copy_sems.at[0])
    fetch_near = pltpu.make_async_copy(jacobian.at[2 - 2 * wall], near, copy_sems.at[1])
    fetch_first = pltpu.make_async_copy(jacobian.at[0], first, copy_sems.at[2])
    fetch_centre.start()
    fetch_near.start()
    fetch_first.start()

    bottom[...] = previous[pl.ds(0, extent, stride=depth), :]
    barrier = pltpu.get_barrier_semaphore()
    for device in (right, left, mirror, across):
        pl.semaphore_signal(barrier, inc=1, device_id=device, device_id_type=MESH)
    pl.semaphore_wait(barrier, 4)

    def send(origin, target, number, device):
        return pltpu.make_async_remote_copy(
            src_ref=origin,
            dst_ref=target,
            send_sem=send_sems.at[number],
            recv_sem=recv_sems.at[number],
            device_id=device,
            device_id_type=MESH,
        )

    to_right = send(previous, from_left, 0, right)
    to_left = send(previous, from_right, 1, left)
    to_mirror = send(bottom, facing, 2, mirror)
    to_right.start()
    to_left.start()
    to_mirror.start()

    lengths = length[...]
    base = wall * depth

    def level_at(step):
        return step + wall * (depth - 1 - 2 * step)

    def mask_at(level):
        return jnp.where(level < lengths, 1.0, 0.0).astype(jnp.float32)

    place = lax.broadcasted_iota(jnp.int32, (extent, lengths.shape[1]), 0)

    def diagonal(step, row):
        level = level_at(step)
        mask = mask_at(level + base)
        block = centre[pl.ds(row * extent * depth + level, extent, stride=depth), :]
        return block * mask + jnp.where(place == row, 1.0 - mask, 0.0)

    fetch_centre.wait()
    for row in range(extent):
        schur[pl.ds(row * extent, extent), :] = diagonal(0, row)
    fetch_near.wait()

    def advance(step, _):
        level = level_at(step)
        start = pl.multiple_of(step * (extent * extent), extent * extent)
        mask = mask_at(level + base + 1 - wall)
        low, high, beyond = [], [], []
        for row in range(extent):
            low.append(schur[pl.ds(start + row * extent, half), :])
            high.append(schur[pl.ds(start + row * extent + half, half), :])
            block = near[pl.ds(row * extent * depth + level, extent, stride=depth), :] * mask
            masked[row * extent : (row + 1) * extent, :] = block
            beyond.append((block[:half], block[half:]))
        sweep(low, high, beyond)
        for row in range(extent):
            inverse[pl.ds(start + row * extent, half), :] = low[row]
            inverse[pl.ds(start + row * extent + half, half), :] = high[row]
            carry[pl.ds(start + row * extent, half), :] = beyond[row][0]
            carry[pl.ds(start + row * extent + half, half), :] = beyond[row][1]
        following = jnp.minimum(step + 1, depth - 1)
        ahead = pl.multiple_of((step + 1) * (extent * extent), extent * extent)
        for row in range(extent):
            change_low, change_high = None, None
            for inner in range(extent):
                factor = jnp.broadcast_to(
                    masked[inner * extent + row : inner * extent + row + 1, :],
                    (half, lengths.shape[1]),
                )
                term_low, term_high = factor * beyond[inner][0], factor * beyond[inner][1]
                change_low = term_low if inner == 0 else change_low + term_low
                change_high = term_high if inner == 0 else change_high + term_high
            block_out[row * extent : row * extent + half, :] = change_low
            block_out[row * extent + half : (row + 1) * extent, :] = change_high
            block = diagonal(following, row)
            schur[pl.ds(ahead + row * extent, half), :] = block[:half] - change_low
            schur[pl.ds(ahead + row * extent + half, half), :] = block[half:] - change_high
        return 0

    lax.fori_loop(0, depth, advance, 0)
    to_across = send(block_out, block_in, 3, across)
    to_across.start()

    fetch_first.wait()
    to_right.wait()
    to_left.wait()
    to_mirror.wait()
    own = previous[...]
    has_left = jnp.where(plane > 0, 1.0, 0.0).astype(jnp.float32)
    has_right = jnp.where(plane < planes - 1, 1.0, 0.0).astype(jnp.float32)
    span = lengths.shape[1]
    offline = (
        coupling[0] * (from_left[...] * has_left)
        + coupling[1] * (from_right[...] * has_right)
        + coupling[2] * pltpu.roll(own, 1, 1)
        + coupling[3] * pltpu.roll(own, span - 1, 1)
    )
    rows = extent * depth
    levels = lax.rem(lax.broadcasted_iota(jnp.int32, (rows, span), 0), depth) + base
    active = jnp.where(levels < lengths, 1.0, 0.0).astype(jnp.float32)
    source[...] = (residual[...] + offline) * active
    chosen = jnp.where(
        lax.broadcasted_iota(jnp.int32, (span, span), 0) == partner_map[...], 1.0, 0.0
    ).astype(jnp.float32)
    partner = jnp.dot(
        facing[...], chosen, precision=lax.Precision.HIGHEST, preferred_element_type=jnp.float32
    )
    wake = total(
        [
            first[pl.ds(inner * depth, extent, stride=extent * depth), :]
            * spread(partner, inner, extent)
            for inner in range(extent)
        ]
    )
    weight = flag[...].astype(jnp.float32) * jnp.where(wall == 0, 1.0, 0.0).astype(jnp.float32)
    bottom_rows = pl.ds(0, extent, stride=depth)
    source[bottom_rows, :] = source[bottom_rows, :] - wake * weight * mask_at(base)

    def source_at(step):
        return source[pl.ds(level_at(step), extent, stride=depth), :]

    reduced[0:extent, :] = source_at(0)

    def forward(step, vector):
        start = pl.multiple_of(step * (extent * extent), extent * extent)
        spreads = [spread(vector, row, extent) for row in range(extent)]
        change = total(
            [spreads[row] * carry[pl.ds(start + row * extent, extent), :] for row in range(extent)]
        )
        given = total(
            [spreads[row] * inverse[pl.ds(start + row * extent, extent), :] for row in range(extent)]
        )
        fixed[pl.ds(pl.multiple_of(step * extent, extent), extent), :] = -given
        vector_out[...] = change
        following = source_at(jnp.minimum(step + 1, depth - 1)) - change
        reduced[pl.ds(pl.multiple_of((step + 1) * extent, extent), extent), :] = following
        return following

    lax.fori_loop(0, depth, forward, source_at(0))
    vector_across = send(vector_out, vector_in, 4, across)
    vector_across.start()

    to_across.wait()
    last = (depth - 1) * extent * extent
    low, high = [], []
    for row in range(extent):
        here = last + row * extent
        low.append(schur[here : here + half, :] - block_in[row * extent : row * extent + half, :])
        high.append(
            schur[here + half : here + extent, :]
            - block_in[row * extent + half : (row + 1) * extent, :]
        )
    sweep(low, high, None)
    vector_across.wait()
    given = reduced[(depth - 1) * extent : depth * extent, :] - vector_in[...]
    spreads = [spread(given, row, half) for row in range(extent)]
    value = -jnp.concatenate(
        [
            total([spreads[row] * low[row] for row in range(extent)]),
            total([spreads[row] * high[row] for row in range(extent)]),
        ],
        axis=0,
    )
    out[pl.ds(level_at(depth - 1), extent, stride=depth), :] = value

    def backward(count, value):
        step = depth - 2 - count
        start = pl.multiple_of(step * (extent * extent), extent * extent)
        change = total(
            [
                spread(value, column, extent)
                * carry[pl.ds(start + column, extent, stride=extent), :]
                for column in range(extent)
            ]
        )
        value = fixed[pl.ds(pl.multiple_of(step * extent, extent), extent), :] - change
        out[pl.ds(level_at(step), extent, stride=depth), :] = value
        return value

    lax.fori_loop(0, depth - 1, backward, value)


def per_device(
    jacobian, residual, previous_update, offline_coupling, wake_partner, line_length, bottom_flag
):
    extent, depth, span = jacobian.shape[1], jacobian.shape[3], jacobian.shape[5]
    block = extent * extent
    whole = pl.BlockSpec(memory_space=pltpu.VMEM)
    f32 = jnp.float32

    def room(rows):
        return pltpu.VMEM((rows, span), f32)

    result = pl.pallas_call(
        functools.partial(kernel, extent, depth),
        out_shape=jax.ShapeDtypeStruct((extent * depth, span), f32),
        in_specs=[pl.BlockSpec(memory_space=pl.ANY)] + [whole] * 6,
        out_specs=whole,
        scratch_shapes=[
            room(block * depth),
            room(block * depth),
            room(block * depth),
            room(block * (depth + 1)),
            room(block * depth),
            room(block * depth),
            room(block),
            room(extent * depth),
            room(extent * (depth + 1)),
            room(extent * depth),
            room(extent),
            room(extent),
            room(extent * depth),
            room(extent * depth),
            room(block),
            room(block),
            room(extent),
            room(extent),
            pltpu.SemaphoreType.DMA((3,)),
            pltpu.SemaphoreType.DMA((5,)),
            pltpu.SemaphoreType.DMA((5,)),
        ],
        compiler_params=pltpu.CompilerParams(
            collective_id=0, has_side_effects=True, vmem_limit_bytes=40 * 1024 * 1024
        ),
    )(
        jacobian.reshape(3, block * depth, span),
        residual.reshape(extent * depth, span),
        previous_update.reshape(extent * depth, span),
        offline_coupling.reshape(4, extent * depth, span),
        wake_partner,
        line_length,
        bottom_flag,
    )
    return result.reshape(extent, depth, 1, span)


def solution(mesh):
    return jax.shard_map(
        per_device,
        mesh=mesh,
        in_specs=(
            P(None, None, None, "wall", "plane", None),
            P(None, "wall", "plane", None),
            P(None, "wall", "plane", None),
            P(None, None, "wall", "plane", None),
            P("plane", None),
            P("plane", None),
            P("plane", None),
        ),
        out_specs=P(None, "wall", "plane", None),
        check_vma=False,
    )
```

time: 597 us -> 30.3 us (0.05); the launches traced: 591 us -> 30 us
  local copies, waits for them, and re-layouts: 331 us -> 8.25 us
  other arithmetic: 108 us -> 0 us
  matrix products: 86.8 us -> 0 us
  blocking collectives: 25.4 us -> 0 us
  loops' own time: 23.4 us -> 0 us
  Pallas kernels: 0 us -> 21.8 us
  starting transfers between devices: 8.53 us -> 0 us
  waiting for transfers between devices: 7.46 us -> 0 us
    dot_general x32 -> x0, matrix products: 86.8 us -> none  [product(): return jnp.einsum('vwc,wuc->vuc', left, right, precision=precise)]
    dynamic_update_slice x112 -> x0, local copies, waits for them, and re-layouts: 86.5 us -> none  [the longest x48 84.8 us: advance(): blocks = lax.dynamic_update_index_in_dim(blocks, block_next, level, 2)]
    slice x89 -> x0, local copies, waits for them, and re-layouts: 58.5 us -> none  [the longest x32 32.9 us: solve_block(): pivot_row = augmented[pivot] / augmented[pivot, pivot][None, :]]
    while x48 -> x0, other arithmetic: 50.4 us -> none
    scatter x512 -> x0, local copies, waits for them, and re-layouts: 44.3 us -> none  [solve_block(): augmented = augmented.at[pivot].set(pivot_row)]
    dynamic_slice x34 -> x0, local copies, waits for them, and re-layouts: 42.5 us -> none  [the longest x32 42.4 us: retreat(): block = lax.dynamic_index_in_dim(blocks, level, 2, keepdims=False)]
    squeeze x34 -> x0, local copies, waits for them, and re-layouts: 30.2 us -> none  [the longest x32 29.3 us: advance(): above = lax.dynamic_index_in_dim(upper, level, 2, keepdims=False)]
    all_gather x1 -> x0, blocking collectives: 25.4 us -> none  [per_device(): whole = lax.all_gather(bottom_row, 'plane', axis=1, tiled=True)]
  transfers between devices with their start and end apart: 4 -> 0, of which waited for: 2 -> 0; matrix products, arithmetic and copies ran while one was open for 10% -> 0% of each run, Pallas kernels for 0% -> 0%
where the time goes in v1:
time: 30.3 us; the launch traced here: 30 us
  Pallas kernels  21.8 us (72%)
  local copies, waits for them, and re-layouts  8.25 us (27%)
    pallas_call x1, Pallas kernels, per_device(): pl.pallas_call(functools.partial(kernel, extent, depth), out_shape=jax.Sh...  21.8 us
    unnamed x15, local copies, waits for them, and re-layouts  8.25 us

profile of v1, /device:TPU:0, one launch (start us, length us, event | category | flops | bytes accessed | tf_op | source)
XLA Modules:
  0.0 30.0 jit_solution(6661159149507533969)
XLA Ops:
  0.0 0.0 copy-start
  0.0 2.8 %copy-done = f32[3,16,16,16,1,128]{5,4,3,2,1,0:T(1,128)S(1)} copy-done((f32[3,16,16,16,1,128]{5,4,3,2,1,0:T(1,128)S(1)}, f32[3,16,16,16,1,128]{5,4,3,2,1,0:T(1,128)}, u32[]{:S(2)}) %copy-start) | copy-done | bytes 6291480
  2.8 0.0 copy-start.1
  2.8 1.0 %copy-done.1 = f32[4,16,16,1,128]{4,3,2,1,0:T(1,128)S(1)} copy-done((f32[4,16,16,1,128]{4,3,2,1,0:T(1,128)S(1)}, f32[4,16,16,1,128]{4,3,2,1,0:T(1,128)}, u32[]{:S(2)}) %copy-start.1) | copy-done | bytes 524312
  3.8 0.0 copy-start.2
  3.8 0.9 %copy-done.2 = f32[16,16,1,128]{3,2,1,0:T(1,128)S(1)} copy-done((f32[16,16,1,128]{3,2,1,0:T(1,128)S(1)}, f32[16,16,1,128]{3,2,1,0:T(1,128)}, u32[]{:S(2)}) %copy-start.2) | copy-done | bytes 131096
  4.7 0.0 copy-start.3
  4.7 0.9 %copy-done.3 = f32[16,16,1,128]{3,2,1,0:T(1,128)S(1)} copy-done((f32[16,16,1,128]{3,2,1,0:T(1,128)S(1)}, f32[16,16,1,128]{3,2,1,0:T(1,128)}, u32[]{:S(2)}) %copy-start.3) | copy-done | bytes 131096
  5.6 0.0 copy-start.4
  5.6 0.7 %copy-done.4 = s32[1,128]{1,0:T(1,128)S(1)} copy-done((s32[1,128]{1,0:T(1,128)S(1)}, s32[1,128]{1,0:T(1,128)}, u32[]{:S(2)}) %copy-start.4) | copy-done | bytes 536
  6.3 0.0 copy-start.5
  6.3 0.7 %copy-done.5 = s32[1,128]{1,0:T(1,128)S(1)} copy-done((s32[1,128]{1,0:T(1,128)S(1)}, s32[1,128]{1,0:T(1,128)}, u32[]{:S(2)}) %copy-start.5) | copy-done | bytes 536
  6.9 0.0 copy-start.6
  7.0 0.7 %copy-done.6 = s32[1,128]{1,0:T(1,128)S(1)} copy-done((s32[1,128]{1,0:T(1,128)S(1)}, s32[1,128]{1,0:T(1,128)}, u32[]{:S(2)}) %copy-start.6) | copy-done | bytes 536
  7.6 21.8 %shard_map.73 = f32[256,128]{1,0:T(8,128)S(1)} custom-call(f32[3,4096,128]{2,1,0:T(8,128)S(1)} %bitcast.7, f32[256,128]{1,0:T(8,128)S(1)} %bitcast.10, f32[256,128]{1,0:T(8,128)S(1)} %bitcast.11, f32[4,256,128]{2,1,0:T(8,128)S(1)} %bitcast.9, s32[1,128]{1,0:T(1,128)S(1)} %copy-done.4, s32[1,128]{1,0:T(1,128)S(1)} %copy-done.5, s32[1,128]{1,0:T(1,128)S(1)} %copy-done.6), custom_call_target="tpu_custom_call" | custom-call | tf_op jit(solution)/shard_map/pallas_call | solution.py:306
  29.4 0.7 %copy.10 = f32[16,16,1,128]{3,2,1,0:T(1,128)} copy(f32[16,16,1,128]{3,2,1,0:T(1,128)S(1)} %bitcast.8) | data formatting | bytes 262144
Async XLA Ops:
  0.0 2.8 %copy-start = (f32[3,16,16,16,1,128]{5,4,3,2,1,0:T(1,128)S(1)}, f32[3,16,16,16,1,128]{5,4,3,2,1,0:T(1,128)}, u32[]{:S(2)}) copy-start(f32[3,16,16,16,1,128]{5,4,3,2,1,0:T(1,128)} %param.7) | copy-start | bytes 18874372
  2.8 1.0 %copy-start.1 = (f32[4,16,16,1,128]{4,3,2,1,0:T(1,128)S(1)}, f32[4,16,16,1,128]{4,3,2,1,0:T(1,128)}, u32[]{:S(2)}) copy-start(f32[4,16,16,1,128]{4,3,2,1,0:T(1,128)} %param.10) | copy-start | bytes 1572868
  3.8 0.9 %copy-start.2 = (f32[16,16,1,128]{3,2,1,0:T(1,128)S(1)}, f32[16,16,1,128]{3,2,1,0:T(1,128)}, u32[]{:S(2)}) copy-start(f32[16,16,1,128]{3,2,1,0:T(1,128)} %param.8) | copy-start | bytes 393220
  4.7 0.9 %copy-start.3 = (f32[16,16,1,128]{3,2,1,0:T(1,128)S(1)}, f32[16,16,1,128]{3,2,1,0:T(1,128)}, u32[]{:S(2)}) copy-start(f32[16,16,1,128]{3,2,1,0:T(1,128)} %param.9) | copy-start | bytes 393220
  5.6 0.7 %copy-start.4 = (s32[1,128]{1,0:T(1,128)S(1)}, s32[1,128]{1,0:T(1,128)}, u32[]{:S(2)}) copy-start(s32[1,128]{1,0:T(1,128)} %partner_map.1) | copy-start | bytes 1540
  6.3 0.7 %copy-start.5 = (s32[1,128]{1,0:T(1,128)S(1)}, s32[1,128]{1,0:T(1,128)}, u32[]{:S(2)}) copy-start(s32[1,128]{1,0:T(1,128)} %length.1) | copy-start | bytes 1540
  6.9 0.7 %copy-start.6 = (s32[1,128]{1,0:T(1,128)S(1)}, s32[1,128]{1,0:T(1,128)}, u32[]{:S(2)}) copy-start(s32[1,128]{1,0:T(1,128)} %flag.1) | copy-start | bytes 1540

commit v2 on v1

--- a/solution.py
+++ b/solution.py
@@ -14,16 +14,24 @@
     return jnp.broadcast_to(row[index : index + 1, :], (rows, row.shape[1]))
 
 
-def sweep(low, high, right):
+def sweep(low, high, right, following):
     extent = len(low)
     half = low[0].shape[0]
+    group = 4
     place = lax.broadcasted_iota(jnp.int32, low[0].shape, 0)
+
+    def entry(row, column):
+        return spread(low[row] if column < half else high[row], column % half, half)
+
+    inverse = 1.0 / entry(0, 0)
+    finished = []
     for pivot in range(extent):
         in_low = pivot < half
-        at = pivot % half
+        here = place == pivot % half
         pivot_low, pivot_high = low[pivot], high[pivot]
-        inverse = 1.0 / spread(pivot_low if in_low else pivot_high, at, half)
-        here = place == at
+        if pivot + 1 < extent:
+            beside = entry(pivot, pivot + 1)
+            next_inverse = 1.0 / (entry(pivot + 1, pivot + 1) - beside * (beside * inverse))
         scaled_low, scaled_high = pivot_low * inverse, pivot_high * inverse
         if in_low:
             scaled_low = jnp.where(here, -inverse, scaled_low)
@@ -31,6 +39,7 @@
             scaled_high = jnp.where(here, -inverse, scaled_high)
         if right is not None:
             scaled_right = tuple(part * inverse for part in right[pivot])
+            finished.append((right[pivot], scaled_right))
         order = [(pivot + 1 + step) % extent for step in range(extent - 1)]
         for row in order:
             factor = spread(pivot_low if row < half else pivot_high, row % half, half)
@@ -48,6 +57,21 @@
         low[pivot], high[pivot] = scaled_low, scaled_high
         if right is not None:
             right[pivot] = scaled_right
+        if len(finished) == group:
+            next_low, next_high = following
+            for row in range(extent):
+                factors = [
+                    spread(plain[row // half], row % half, half) for plain, _ in finished
+                ]
+                if row < half:
+                    next_low[row] = next_low[row] - total(
+                        [factor * scaled[0] for factor, (_, scaled) in zip(factors, finished)]
+                    )
+                next_high[row] = next_high[row] - total(
+                    [factor * scaled[1] for factor, (_, scaled) in zip(factors, finished)]
+                )
+            finished = []
+        inverse = next_inverse
 
 
 def total(terms):
@@ -63,20 +87,25 @@
     extent,
     depth,
     jacobian,
+    residual_far,
+    previous_far,
+    coupling_far,
+    partner_far,
+    length_far,
+    flag_far,
+    out,
     residual,
     previous,
     coupling,
     partner_map,
     length,
     flag,
-    out,
-    near,
-    centre,
+    near_store,
+    centre_store,
     first,
     schur,
     inverse,
     carry,
-    masked,
     source,
     reduced,
     fixed,
@@ -101,12 +130,40 @@
     mirror = {"wall": wall, "plane": lax.rem(plane + planes // 2, planes)}
     across = {"wall": 1 - wall, "plane": plane}
 
-    fetch_centre = pltpu.make_async_copy(jacobian.at[1], centre, copy_sems.at[0])
-    fetch_near = pltpu.make_async_copy(jacobian.at[2 - 2 * wall], near, copy_sems.at[1])
-    fetch_first = pltpu.make_async_copy(jacobian.at[0], first, copy_sems.at[2])
-    fetch_centre.start()
-    fetch_near.start()
-    fetch_first.start()
+    near = near_store.reshape(extent * extent * depth, near_store.shape[2])
+    centre = centre_store.reshape(extent * extent * depth, near_store.shape[2])
+    middle = depth // 2
+    halves = [pl.multiple_of(wall * middle, middle), pl.multiple_of((1 - wall) * middle, middle)]
+    near_at = 2 - 2 * wall
+    fetches = [
+        pltpu.make_async_copy(previous_far, previous, copy_sems.at[0]),
+        pltpu.make_async_copy(length_far, length, copy_sems.at[1]),
+    ]
+    for at, part in enumerate(halves):
+        levels_here = pl.ds(part, middle)
+        fetches.append(
+            pltpu.make_async_copy(
+                jacobian.at[1, :, levels_here], centre_store.at[:, levels_here], copy_sems.at[2 + 2 * at]
+            )
+        )
+        fetches.append(
+            pltpu.make_async_copy(
+                jacobian.at[near_at, :, levels_here],
+                near_store.at[:, levels_here],
+                copy_sems.at[3 + 2 * at],
+            )
+        )
+    late = [
+        pltpu.make_async_copy(jacobian.at[0, :, pl.ds(0, middle)], first, copy_sems.at[6]),
+        pltpu.make_async_copy(residual_far, residual, copy_sems.at[7]),
+        pltpu.make_async_copy(coupling_far, coupling, copy_sems.at[8]),
+        pltpu.make_async_copy(partner_far, partner_map, copy_sems.at[9]),
+        pltpu.make_async_copy(flag_far, flag, copy_sems.at[10]),
+    ]
+    for fetch in fetches + late:
+        fetch.start()
+    fetches[0].wait()
+    fetches[1].wait()
 
     bottom[...] = previous[pl.ds(0, extent, stride=depth), :]
     barrier = pltpu.get_barrier_semaphore()
@@ -148,52 +205,57 @@
         block = centre[pl.ds(row * extent * depth + level, extent, stride=depth), :]
         return block * mask + jnp.where(place == row, 1.0 - mask, 0.0)
 
-    fetch_centre.wait()
+    fetches[2].wait()
     for row in range(extent):
         schur[pl.ds(row * extent, extent), :] = diagonal(0, row)
-    fetch_near.wait()
+    fetches[3].wait()
 
     def advance(step, _):
         level = level_at(step)
         start = pl.multiple_of(step * (extent * extent), extent * extent)
         mask = mask_at(level + base + 1 - wall)
         low, high, beyond = [], [], []
+        next_low, next_high = [], []
+        following = jnp.minimum(step + 1, depth - 1)
+        kept = jnp.where(step < depth - 1, 1.0, 0.0).astype(jnp.float32)
         for row in range(extent):
-            low.append(schur[pl.ds(start + row * extent, half), :])
+            if row < half:
+                low.append(schur[pl.ds(start + row * extent, half), :])
+            else:
+                low.append(schur[pl.ds(start + row, half, stride=extent), :])
             high.append(schur[pl.ds(start + row * extent + half, half), :])
             block = near[pl.ds(row * extent * depth + level, extent, stride=depth), :] * mask
-            masked[row * extent : (row + 1) * extent, :] = block
             beyond.append((block[:half], block[half:]))
-        sweep(low, high, beyond)
+            block = diagonal(following, row) * kept
+            next_low.append(block[:half])
+            next_high.append(block[half:])
+        sweep(low, high, beyond, (next_low, next_high))
+        ahead = pl.multiple_of((step + 1) * (extent * extent), extent * extent)
         for row in range(extent):
             inverse[pl.ds(start + row * extent, half), :] = low[row]
             inverse[pl.ds(start + row * extent + half, half), :] = high[row]
             carry[pl.ds(start + row * extent, half), :] = beyond[row][0]
             carry[pl.ds(start + row * extent + half, half), :] = beyond[row][1]
-        following = jnp.minimum(step + 1, depth - 1)
-        ahead = pl.multiple_of((step + 1) * (extent * extent), extent * extent)
-        for row in range(extent):
-            change_low, change_high = None, None
-            for inner in range(extent):
-                factor = jnp.broadcast_to(
-                    masked[inner * extent + row : inner * extent + row + 1, :],
-                    (half, lengths.shape[1]),
-                )
-                term_low, term_high = factor * beyond[inner][0], factor * beyond[inner][1]
-                change_low = term_low if inner == 0 else change_low + term_low
-                change_high = term_high if inner == 0 else change_high + term_high
-            block_out[row * extent : row * extent + half, :] = change_low
-            block_out[row * extent + half : (row + 1) * extent, :] = change_high
-            block = diagonal(following, row)
-            schur[pl.ds(ahead + row * extent, half), :] = block[:half] - change_low
-            schur[pl.ds(ahead + row * extent + half, half), :] = block[half:] - change_high
+            if row < half:
+                schur[pl.ds(ahead + row * extent, half), :] = next_low[row]
+            schur[pl.ds(ahead + row * extent + half, half), :] = next_high[row]
         return 0
 
-    lax.fori_loop(0, depth, advance, 0)
+    lax.fori_loop(0, middle - 1, advance, 0)
+    fetches[4].wait()
+    fetches[5].wait()
+    lax.fori_loop(middle - 1, depth, advance, 0)
+    done = depth * extent * extent
+    upper = half * extent
+    block_out[0:upper, :] = schur[done : done + upper, :]
+    for row in range(half):
+        here = done + (half + row) * extent + half
+        block_out[upper + row * half : upper + (row + 1) * half, :] = schur[here : here + half, :]
     to_across = send(block_out, block_in, 3, across)
     to_across.start()
 
-    fetch_first.wait()
+    for fetch in late:
+        fetch.wait()
     to_right.wait()
     to_left.wait()
     to_mirror.wait()
@@ -217,9 +279,10 @@
     partner = jnp.dot(
         facing[...], chosen, precision=lax.Precision.HIGHEST, preferred_element_type=jnp.float32
     )
+    first_rows = first.reshape(extent * extent * middle, span)
     wake = total(
         [
-            first[pl.ds(inner * depth, extent, stride=extent * depth), :]
+            first_rows[pl.ds(inner * middle, extent, stride=extent * middle), :]
             * spread(partner, inner, extent)
             for inner in range(extent)
         ]
@@ -257,12 +320,20 @@
     low, high = [], []
     for row in range(extent):
         here = last + row * extent
-        low.append(schur[here : here + half, :] - block_in[row * extent : row * extent + half, :])
-        high.append(
-            schur[here + half : here + extent, :]
-            - block_in[row * extent + half : (row + 1) * extent, :]
-        )
-    sweep(low, high, None)
+        if row < half:
+            low.append(schur[here : here + half, :] + block_in[row * extent : row * extent + half, :])
+            high.append(
+                schur[here + half : here + extent, :]
+                + block_in[row * extent + half : (row + 1) * extent, :]
+            )
+        else:
+            low.append(
+                schur[pl.ds(last + row, half, stride=extent), :]
+                + block_in[pl.ds(row, half, stride=extent), :]
+            )
+            at = upper + (row - half) * half
+            high.append(schur[here + half : here + extent, :] + block_in[at : at + half, :])
+    sweep(low, high, None, None)
     vector_across.wait()
     given = reduced[(depth - 1) * extent : depth * extent, :] - vector_in[...]
     spreads = [spread(given, row, half) for row in range(extent)]
@@ -306,16 +377,21 @@
     result = pl.pallas_call(
         functools.partial(kernel, extent, depth),
         out_shape=jax.ShapeDtypeStruct((extent * depth, span), f32),
-        in_specs=[pl.BlockSpec(memory_space=pl.ANY)] + [whole] * 6,
+        in_specs=[pl.BlockSpec(memory_space=pl.ANY)] * 7,
         out_specs=whole,
         scratch_shapes=[
-            room(block * depth),
-            room(block * depth),
-            room(block * depth),
+            room(extent * depth),
+            room(extent * depth),
+            pltpu.VMEM((4, extent * depth, span), f32),
+            pltpu.VMEM((1, span), jnp.int32),
+            pltpu.VMEM((1, span), jnp.int32),
+            pltpu.VMEM((1, span), jnp.int32),
+            pltpu.VMEM((block, depth, span), f32),
+            pltpu.VMEM((block, depth, span), f32),
+            pltpu.VMEM((block, depth // 2, span), f32),
             room(block * (depth + 1)),
             room(block * depth),
             room(block * depth),
-            room(block),
             room(extent * depth),
             room(extent * (depth + 1)),
             room(extent * depth),
@@ -323,19 +399,19 @@
             room(extent),
             room(extent * depth),
             room(extent * depth),
-            room(block),
-            room(block),
+            room(block * 3 // 4),
+            room(block * 3 // 4),
             room(extent),
             room(extent),
-            pltpu.SemaphoreType.DMA((3,)),
+            pltpu.SemaphoreType.DMA((11,)),
             pltpu.SemaphoreType.DMA((5,)),
             pltpu.SemaphoreType.DMA((5,)),
         ],
         compiler_params=pltpu.CompilerParams(
-            collective_id=0, has_side_effects=True, vmem_limit_bytes=40 * 1024 * 1024
+            collective_id=0, has_side_effects=True, vmem_limit_bytes=63 * 1024 * 1024
         ),
     )(
-        jacobian.reshape(3, block * depth, span),
+        jacobian.reshape(3, block, depth, span),
         residual.reshape(extent * depth, span),
         previous_update.reshape(extent * depth, span),
         offline_coupling.reshape(4, extent * depth, span),

time: 30.3 us -> 23.9 us (0.79)
  local copies, waits for them, and re-layouts: 8.25 us -> 1.57 us
    unnamed x15 -> x1, local copies, waits for them, and re-layouts: 8.25 us -> 1.57 us
    pallas_call x1, Pallas kernels: 21.8 us -> 22.1 us  [per_device(): pl.pallas_call(functools.partial(kernel, extent, depth), out_shape=jax.Sh...]
where the time goes in v2:
time: 23.9 us; the launch traced here: 23.7 us
  Pallas kernels  22.1 us (92%)
  local copies, waits for them, and re-layouts  1.57 us (7%)
    pallas_call x1, Pallas kernels, per_device(): pl.pallas_call(functools.partial(kernel, extent, depth), out_shape=jax.Sh...  22.1 us
    unnamed x1, local copies, waits for them, and re-layouts  1.57 us

profile of v2, /device:TPU:0, one launch (start us, length us, event | category | flops | bytes accessed | tf_op | source)
XLA Modules:
  0.0 23.7 jit_solution(8824677749184718210)
XLA Ops:
  0.0 22.1 %shard_map.73 = f32[256,128]{1,0:T(8,128)} custom-call(f32[3,256,16,128]{3,2,1,0:T(8,128)} %bitcast.7, f32[256,128]{1,0:T(8,128)} %bitcast.10, f32[256,128]{1,0:T(8,128)} %bitcast.11, f32[4,256,128]{2,1,0:T(8,128)} %bitcast.9, s32[1,128]{1,0:T(1,128)} %partner_far.1, s32[1,128]{1,0:T(1,128)} %length_far.1, s32[1,128]{1,0:T(1,128)} %flag_far.1), custom_call_target="tpu_custom_call" | custom-call | tf_op jit(solution)/shard_map/pallas_call | solution.py:377
  22.1 1.6 %copy.10 = f32[16,16,1,128]{3,2,1,0:T(1,128)} copy(f32[16,16,1,128]{3,2,1,0:T(1,128)} %bitcast.8) | data formatting | bytes 262144

commit v3 on v2

--- a/solution.py
+++ b/solution.py
@@ -14,11 +14,12 @@
     return jnp.broadcast_to(row[index : index + 1, :], (rows, row.shape[1]))
 
 
-def sweep(low, high, right, following):
-    extent = len(low)
-    half = low[0].shape[0]
+def factor(low, high, right, following):
+    extent = len(high)
+    half = high[0].shape[0]
     group = 4
-    place = lax.broadcasted_iota(jnp.int32, low[0].shape, 0)
+    place = lax.broadcasted_iota(jnp.int32, high[0].shape, 0)
+    scales = [jnp.zeros_like(high[0]), jnp.zeros_like(high[0])]
 
     def entry(row, column):
         return spread(low[row] if column < half else high[row], column % half, half)
@@ -27,51 +28,55 @@
     finished = []
     for pivot in range(extent):
         in_low = pivot < half
-        here = place == pivot % half
+        at = pivot % half
+        here = place == at
         pivot_low, pivot_high = low[pivot], high[pivot]
         if pivot + 1 < extent:
             beside = entry(pivot, pivot + 1)
             next_inverse = 1.0 / (entry(pivot + 1, pivot + 1) - beside * (beside * inverse))
+        scales[pivot // half] = jnp.where(here, inverse, scales[pivot // half])
         scaled_low, scaled_high = pivot_low * inverse, pivot_high * inverse
         if in_low:
-            scaled_low = jnp.where(here, -inverse, scaled_low)
+            scaled_low = jnp.where(here, inverse, scaled_low)
+            known_low = jnp.where(place <= at, scaled_low, 0.0)
+            low[pivot] = jnp.where(place < at, pivot_low, jnp.where(here, 1.0, 0.0))
+            high[pivot] = None
         else:
-            scaled_high = jnp.where(here, -inverse, scaled_high)
+            scaled_high = jnp.where(here, inverse, scaled_high)
+            high[pivot] = jnp.where(place < at, pivot_high, jnp.where(here, 1.0, 0.0))
         if right is not None:
             scaled_right = tuple(part * inverse for part in right[pivot])
             finished.append((right[pivot], scaled_right))
-        order = [(pivot + 1 + step) % extent for step in range(extent - 1)]
-        for row in order:
-            factor = spread(pivot_low if row < half else pivot_high, row % half, half)
-            kept_low, kept_high = low[row], high[row]
-            if in_low:
-                kept_low = jnp.where(here, 0.0, kept_low)
+            right[pivot] = scaled_right
+        for row in range(pivot + 1, extent):
+            by = spread(pivot_low if row < half else pivot_high, row % half, half)
+            if row < half:
+                low[row] = jnp.where(here, 0.0, low[row]) - by * scaled_low
+                high[row] = high[row] - by * scaled_high
+            elif in_low:
+                low[row] = -(by * known_low) if pivot == 0 else low[row] - by * known_low
+                high[row] = high[row] - by * scaled_high
             else:
-                kept_high = jnp.where(here, 0.0, kept_high)
-            low[row] = kept_low - factor * scaled_low
-            high[row] = kept_high - factor * scaled_high
+                low[row] = low[row] - by * scaled_low
+                high[row] = jnp.where(here, 0.0, high[row]) - by * scaled_high
             if right is not None:
                 right[row] = tuple(
-                    part - factor * scaled for part, scaled in zip(right[row], scaled_right)
+                    part - by * scaled for part, scaled in zip(right[row], scaled_right)
                 )
-        low[pivot], high[pivot] = scaled_low, scaled_high
-        if right is not None:
-            right[pivot] = scaled_right
         if len(finished) == group:
             next_low, next_high = following
             for row in range(extent):
-                factors = [
-                    spread(plain[row // half], row % half, half) for plain, _ in finished
-                ]
+                bys = [spread(plain[row // half], row % half, half) for plain, _ in finished]
                 if row < half:
                     next_low[row] = next_low[row] - total(
-                        [factor * scaled[0] for factor, (_, scaled) in zip(factors, finished)]
+                        [by * scaled[0] for by, (_, scaled) in zip(bys, finished)]
                     )
                 next_high[row] = next_high[row] - total(
-                    [factor * scaled[1] for factor, (_, scaled) in zip(factors, finished)]
+                    [by * scaled[1] for by, (_, scaled) in zip(bys, finished)]
                 )
             finished = []
         inverse = next_inverse
+    return scales
 
 
 def total(terms):
@@ -109,6 +114,7 @@
     source,
     reduced,
     fixed,
+    scale,
     bottom,
     facing,
     from_left,
@@ -169,6 +175,61 @@
     barrier = pltpu.get_barrier_semaphore()
     for device in (right, left, mirror, across):
         pl.semaphore_signal(barrier, inc=1, device_id=device, device_id_type=MESH)
+    lengths = length[...]
+    base = wall * depth
+
+    def level_at(step):
+        return step + wall * (depth - 1 - 2 * step)
+
+    def mask_at(level):
+        return jnp.where(level < lengths, 1.0, 0.0).astype(jnp.float32)
+
+    place = lax.broadcasted_iota(jnp.int32, (extent, lengths.shape[1]), 0)
+
+    def diagonal(step, row):
+        level = level_at(step)
+        mask = mask_at(level + base)
+        block = centre[pl.ds(row * extent * depth + level, extent, stride=depth), :]
+        return block * mask + jnp.where(place == row, 1.0 - mask, 0.0)
+
+    fetches[2].wait()
+    for row in range(extent):
+        schur[pl.ds(row * extent, extent), :] = diagonal(0, row)
+    fetches[3].wait()
+
+    def advance(step, _):
+        level = level_at(step)
+        start = pl.multiple_of(step * (extent * extent), extent * extent)
+        mask = mask_at(level + base + 1 - wall)
+        low, high, beyond = [], [], []
+        next_low, next_high = [], []
+        following = jnp.minimum(step + 1, depth - 1)
+        kept = jnp.where(step < depth - 1, 1.0, 0.0).astype(jnp.float32)
+        for row in range(extent):
+            low.append(schur[pl.ds(start + row * extent, half), :] if row < half else None)
+            high.append(schur[pl.ds(start + row * extent + half, half), :])
+            block = near[pl.ds(row * extent * depth + level, extent, stride=depth), :] * mask
+            beyond.append((block[:half], block[half:]))
+            block = diagonal(following, row) * kept
+            next_low.append(block[:half])
+            next_high.append(block[half:])
+        scales = factor(low, high, beyond, (next_low, next_high))
+        ahead = pl.multiple_of((step + 1) * (extent * extent), extent * extent)
+        scale_at = pl.multiple_of(step * extent, extent)
+        scale[pl.ds(scale_at, half), :] = scales[0]
+        scale[pl.ds(scale_at + half, half), :] = scales[1]
+        for row in range(extent):
+            inverse[pl.ds(start + row * extent, half), :] = low[row]
+            if row >= half:
+                inverse[pl.ds(start + row * extent + half, half), :] = high[row]
+            carry[pl.ds(start + row * extent, half), :] = beyond[row][0]
+            carry[pl.ds(start + row * extent + half, half), :] = beyond[row][1]
+            if row < half:
+                schur[pl.ds(ahead + row * extent, half), :] = next_low[row]
+            schur[pl.ds(ahead + row * extent + half, half), :] = next_high[row]
+        return 0
+
+    lax.fori_loop(0, middle - 1, advance, 0)
     pl.semaphore_wait(barrier, 4)
 
     def send(origin, target, number, device):
@@ -188,60 +249,6 @@
     to_left.start()
     to_mirror.start()
 
-    lengths = length[...]
-    base = wall * depth
-
-    def level_at(step):
-        return step + wall * (depth - 1 - 2 * step)
-
-    def mask_at(level):
-        return jnp.where(level < lengths, 1.0, 0.0).astype(jnp.float32)
-
-    place = lax.broadcasted_iota(jnp.int32, (extent, lengths.shape[1]), 0)
-
-    def diagonal(step, row):
-        level = level_at(step)
-        mask = mask_at(level + base)
-        block = centre[pl.ds(row * extent * depth + level, extent, stride=depth), :]
-        return block * mask + jnp.where(place == row, 1.0 - mask, 0.0)
-
-    fetches[2].wait()
-    for row in range(extent):
-        schur[pl.ds(row * extent, extent), :] = diagonal(0, row)
-    fetches[3].wait()
-
-    def advance(step, _):
-        level = level_at(step)
-        start = pl.multiple_of(step * (extent * extent), extent * extent)
-        mask = mask_at(level + base + 1 - wall)
-        low, high, beyond = [], [], []
-        next_low, next_high = [], []
-        following = jnp.minimum(step + 1, depth - 1)
-        kept = jnp.where(step < depth - 1, 1.0, 0.0).astype(jnp.float32)
-        for row in range(extent):
-            if row < half:
-                low.append(schur[pl.ds(start + row * extent, half), :])
-            else:
-                low.append(schur[pl.ds(start + row, half, stride=extent), :])
-            high.append(schur[pl.ds(start + row * extent + half, half), :])
-            block = near[pl.ds(row * extent * depth + level, extent, stride=depth), :] * mask
-            beyond.append((block[:half], block[half:]))
-            block = diagonal(following, row) * kept
-            next_low.append(block[:half])
-            next_high.append(block[half:])
-        sweep(low, high, beyond, (next_low, next_high))
-        ahead = pl.multiple_of((step + 1) * (extent * extent), extent * extent)
-        for row in range(extent):
-            inverse[pl.ds(start + row * extent, half), :] = low[row]
-            inverse[pl.ds(start + row * extent + half, half), :] = high[row]
-            carry[pl.ds(start + row * extent, half), :] = beyond[row][0]
-            carry[pl.ds(start + row * extent + half, half), :] = beyond[row][1]
-            if row < half:
-                schur[pl.ds(ahead + row * extent, half), :] = next_low[row]
-            schur[pl.ds(ahead + row * extent + half, half), :] = next_high[row]
-        return 0
-
-    lax.fori_loop(0, middle - 1, advance, 0)
     fetches[4].wait()
     fetches[5].wait()
     lax.fori_loop(middle - 1, depth, advance, 0)
@@ -294,24 +301,69 @@
     def source_at(step):
         return source[pl.ds(level_at(step), extent, stride=depth), :]
 
-    reduced[0:extent, :] = source_at(0)
+    def halves_of(vector):
+        return vector[:half], vector[half:]
+
+    def spreads_of(vector):
+        return [spread(vector[row // half], row % half, half) for row in range(extent)]
+
+    def by_rows(spreads, store, start):
+        return [
+            total(
+                [
+                    spreads[row] * store[pl.ds(start + row * extent + part * half, half), :]
+                    for row in range(extent)
+                ]
+            )
+            for part in range(2)
+        ]
+
+    def by_columns(spreads, store, start):
+        return [
+            total(
+                [
+                    spreads[column]
+                    * store[
+                        pl.ds(start + part * half * extent + column, half, stride=extent), :
+                    ]
+                    for column in range(extent)
+                ]
+            )
+            for part in range(2)
+        ]
+
+    def lower_rows(rows_low, rows_high, spreads):
+        return [
+            total([spreads[row] * rows_low(row) for row in range(extent)]),
+            total([spreads[row] * rows_high(row) for row in range(half, extent)]),
+        ]
 
     def forward(step, vector):
         start = pl.multiple_of(step * (extent * extent), extent * extent)
-        spreads = [spread(vector, row, extent) for row in range(extent)]
-        change = total(
-            [spreads[row] * carry[pl.ds(start + row * extent, extent), :] for row in range(extent)]
-        )
-        given = total(
-            [spreads[row] * inverse[pl.ds(start + row * extent, extent), :] for row in range(extent)]
-        )
-        fixed[pl.ds(pl.multiple_of(step * extent, extent), extent), :] = -given
-        vector_out[...] = change
-        following = source_at(jnp.minimum(step + 1, depth - 1)) - change
-        reduced[pl.ds(pl.multiple_of((step + 1) * extent, extent), extent), :] = following
-        return following
-
-    lax.fori_loop(0, depth, forward, source_at(0))
+        at = pl.multiple_of(step * extent, extent)
+        reduced[pl.ds(at, half), :] = vector[0]
+        reduced[pl.ds(at + half, half), :] = vector[1]
+        spreads = spreads_of(vector)
+        lifted = [
+            total(
+                [
+                    spreads[column]
+                    * inverse[pl.ds(start + part * half * extent + column, half, stride=extent), :]
+                    for column in range(half * (part + 1))
+                ]
+            )
+            for part in range(2)
+        ]
+        for part in range(2):
+            here = pl.ds(at + part * half, half)
+            fixed[here, :] = lifted[part] * scale[here, :]
+        change = by_rows(spreads_of(lifted), carry, start)
+        vector_out[0:half, :] = change[0]
+        vector_out[half:extent, :] = change[1]
+        following = halves_of(source_at(jnp.minimum(step + 1, depth - 1)))
+        return tuple(given - less for given, less in zip(following, change))
+
+    lax.fori_loop(0, depth, forward, halves_of(source_at(0)))
     vector_across = send(vector_out, vector_in, 4, across)
     vector_across.start()
 
@@ -327,40 +379,55 @@
                 + block_in[row * extent + half : (row + 1) * extent, :]
             )
         else:
-            low.append(
-                schur[pl.ds(last + row, half, stride=extent), :]
-                + block_in[pl.ds(row, half, stride=extent), :]
-            )
+            low.append(None)
             at = upper + (row - half) * half
             high.append(schur[here + half : here + extent, :] + block_in[at : at + half, :])
-    sweep(low, high, None, None)
+    scales = factor(low, high, None, None)
+    for row in range(extent):
+        inverse[last + row * extent : last + row * extent + half, :] = low[row]
+        if row >= half:
+            inverse[last + row * extent + half : last + (row + 1) * extent, :] = high[row]
     vector_across.wait()
-    given = reduced[(depth - 1) * extent : depth * extent, :] - vector_in[...]
-    spreads = [spread(given, row, half) for row in range(extent)]
-    value = -jnp.concatenate(
-        [
-            total([spreads[row] * low[row] for row in range(extent)]),
-            total([spreads[row] * high[row] for row in range(extent)]),
-        ],
-        axis=0,
+    spreads = spreads_of(
+        halves_of(reduced[(depth - 1) * extent : depth * extent, :] - vector_in[...])
     )
-    out[pl.ds(level_at(depth - 1), extent, stride=depth), :] = value
+    lifted = [
+        total(
+            [
+                spreads[column]
+                * inverse[pl.ds(last + part * half * extent + column, half, stride=extent), :]
+                for column in range(half * (part + 1))
+            ]
+        )
+        * scales[part]
+        for part in range(2)
+    ]
+
+    def lowered(vector, start):
+        return lower_rows(
+            lambda row: inverse[pl.ds(start + row * extent, half), :],
+            lambda row: inverse[pl.ds(start + row * extent + half, half), :],
+            spreads_of(vector),
+        )
+
+    def put(step, value):
+        out[pl.ds(level_at(step), half, stride=depth), :] = value[0]
+        out[pl.ds(level_at(step) + half * depth, half, stride=depth), :] = value[1]
+
+    value = lowered(lifted, last)
+    put(depth - 1, value)
 
     def backward(count, value):
         step = depth - 2 - count
         start = pl.multiple_of(step * (extent * extent), extent * extent)
-        change = total(
-            [
-                spread(value, column, extent)
-                * carry[pl.ds(start + column, extent, stride=extent), :]
-                for column in range(extent)
-            ]
-        )
-        value = fixed[pl.ds(pl.multiple_of(step * extent, extent), extent), :] - change
-        out[pl.ds(level_at(step), extent, stride=depth), :] = value
-        return value
-
-    lax.fori_loop(0, depth - 1, backward, value)
+        at = pl.multiple_of(step * extent, extent)
+        change = by_columns(spreads_of(value), carry, start)
+        given = [fixed[pl.ds(at + part * half, half), :] - change[part] for part in range(2)]
+        value = lowered(given, start)
+        put(step, value)
+        return tuple(value)
+
+    lax.fori_loop(0, depth - 1, backward, tuple(value))
 
 
 def per_device(
@@ -393,7 +460,8 @@
             room(block * depth),
             room(block * depth),
             room(extent * depth),
-            room(extent * (depth + 1)),
+            room(extent * depth),
+            room(extent * depth),
             room(extent * depth),
             room(extent),
             room(extent),

time: 23.9 us -> 20.3 us (0.85)
  Pallas kernels: 22.1 us -> 18.5 us
    pallas_call x1, Pallas kernels: 22.1 us -> 18.5 us  [per_device(): pl.pallas_call(functools.partial(kernel, extent, depth), out_shape=jax.Sh...]
where the time goes in v3:
time: 20.3 us; the launch traced here: 20.1 us
  Pallas kernels  18.5 us (91%)
  local copies, waits for them, and re-layouts  1.57 us (8%)
    pallas_call x1, Pallas kernels, per_device(): pl.pallas_call(functools.partial(kernel, extent, depth), out_shape=jax.Sh...  18.5 us
    unnamed x1, local copies, waits for them, and re-layouts  1.57 us

profile of v3, /device:TPU:0, one launch (start us, length us, event | category | flops | bytes accessed | tf_op | source)
XLA Modules:
  0.0 20.1 jit_solution(5996724400891387695)
XLA Ops:
  0.0 18.5 %shard_map.73 = f32[256,128]{1,0:T(8,128)} custom-call(f32[3,256,16,128]{3,2,1,0:T(8,128)} %bitcast.7, f32[256,128]{1,0:T(8,128)} %bitcast.10, f32[256,128]{1,0:T(8,128)} %bitcast.11, f32[4,256,128]{2,1,0:T(8,128)} %bitcast.9, s32[1,128]{1,0:T(1,128)} %partner_far.1, s32[1,128]{1,0:T(1,128)} %length_far.1, s32[1,128]{1,0:T(1,128)} %flag_far.1), custom_call_target="tpu_custom_call" | custom-call | tf_op jit(solution)/shard_map/pallas_call | solution.py:444
  18.5 1.6 %copy.10 = f32[16,16,1,128]{3,2,1,0:T(1,128)} copy(f32[16,16,1,128]{3,2,1,0:T(1,128)} %bitcast.8) | data formatting | bytes 262144

commit v4 on v3

--- a/solution.py
+++ b/solution.py
@@ -131,8 +131,9 @@
     plane = lax.axis_index("plane")
     planes = lax.axis_size("plane")
     half = extent // 2
-    right = {"wall": wall, "plane": lax.rem(plane + 1, planes)}
-    left = {"wall": wall, "plane": lax.rem(plane + planes - 1, planes)}
+    has_left, has_right = plane > 0, plane < planes - 1
+    right = {"wall": wall, "plane": plane + 1}
+    left = {"wall": wall, "plane": plane - 1}
     mirror = {"wall": wall, "plane": lax.rem(plane + planes // 2, planes)}
     across = {"wall": 1 - wall, "plane": plane}
 
@@ -159,22 +160,56 @@
                 copy_sems.at[3 + 2 * at],
             )
         )
+    first_fetch = pltpu.make_async_copy(
+        jacobian.at[0, :, pl.ds(0, middle)], first, copy_sems.at[6]
+    )
     late = [
-        pltpu.make_async_copy(jacobian.at[0, :, pl.ds(0, middle)], first, copy_sems.at[6]),
         pltpu.make_async_copy(residual_far, residual, copy_sems.at[7]),
         pltpu.make_async_copy(coupling_far, coupling, copy_sems.at[8]),
         pltpu.make_async_copy(partner_far, partner_map, copy_sems.at[9]),
         pltpu.make_async_copy(flag_far, flag, copy_sems.at[10]),
     ]
-    for fetch in fetches + late:
-        fetch.start()
-    fetches[0].wait()
+    fetches[1].start()
+    fetches[2].start()
+    fetches[3].start()
+    fetches[0].start()
+
+    barrier = pltpu.get_barrier_semaphore()
+
+    def greet(device):
+        pl.semaphore_signal(barrier, inc=1, device_id=device, device_id_type=MESH)
+
+    greet(across)
+    pl.when(wall == 0)(lambda: greet(mirror))
+    pl.when(has_left)(lambda: greet(left))
+    pl.when(has_right)(lambda: greet(right))
+    greetings = (
+        1 + (wall == 0).astype(jnp.int32) + has_left.astype(jnp.int32) + has_right.astype(jnp.int32)
+    )
+
+    @pl.when(jnp.logical_not(has_left))
+    def _():
+        from_left[...] = jnp.zeros_like(from_left)
+
+    @pl.when(jnp.logical_not(has_right))
+    def _():
+        from_right[...] = jnp.zeros_like(from_right)
+
+    def send(origin, target, number, device):
+        return pltpu.make_async_remote_copy(
+            src_ref=origin,
+            dst_ref=target,
+            send_sem=send_sems.at[number],
+            recv_sem=recv_sems.at[number],
+            device_id=device,
+            device_id_type=MESH,
+        )
+
+    to_right = send(previous, from_left, 0, right)
+    to_left = send(previous, from_right, 1, left)
+    to_mirror = send(bottom, facing, 2, mirror)
     fetches[1].wait()
 
-    bottom[...] = previous[pl.ds(0, extent, stride=depth), :]
-    barrier = pltpu.get_barrier_semaphore()
-    for device in (right, left, mirror, across):
-        pl.semaphore_signal(barrier, inc=1, device_id=device, device_id_type=MESH)
     lengths = length[...]
     base = wall * depth
 
@@ -196,8 +231,27 @@
     for row in range(extent):
         schur[pl.ds(row * extent, extent), :] = diagonal(0, row)
     fetches[3].wait()
+    fetches[4].start()
+    fetches[5].start()
+    pl.when(wall == 0)(first_fetch.start)
+    for fetch in late:
+        fetch.start()
+    fetches[0].wait()
+    bottom[...] = previous[pl.ds(0, extent, stride=depth), :]
 
     def advance(step, _):
+        @pl.when(step == 3)
+        def _():
+            pl.semaphore_wait(barrier, greetings)
+            pl.when(has_right)(to_right.start)
+            pl.when(has_left)(to_left.start)
+            pl.when(wall == 0)(to_mirror.start)
+
+        @pl.when(step == middle - 1)
+        def _():
+            fetches[4].wait()
+            fetches[5].wait()
+
         level = level_at(step)
         start = pl.multiple_of(step * (extent * extent), extent * extent)
         mask = mask_at(level + base + 1 - wall)
@@ -229,29 +283,7 @@
             schur[pl.ds(ahead + row * extent + half, half), :] = next_high[row]
         return 0
 
-    lax.fori_loop(0, middle - 1, advance, 0)
-    pl.semaphore_wait(barrier, 4)
-
-    def send(origin, target, number, device):
-        return pltpu.make_async_remote_copy(
-            src_ref=origin,
-            dst_ref=target,
-            send_sem=send_sems.at[number],
-            recv_sem=recv_sems.at[number],
-            device_id=device,
-            device_id_type=MESH,
-        )
-
-    to_right = send(previous, from_left, 0, right)
-    to_left = send(previous, from_right, 1, left)
-    to_mirror = send(bottom, facing, 2, mirror)
-    to_right.start()
-    to_left.start()
-    to_mirror.start()
-
-    fetches[4].wait()
-    fetches[5].wait()
-    lax.fori_loop(middle - 1, depth, advance, 0)
+    lax.fori_loop(0, depth, advance, 0)
     done = depth * extent * extent
     upper = half * extent
     block_out[0:upper, :] = schur[done : done + upper, :]
@@ -263,16 +295,22 @@
 
     for fetch in late:
         fetch.wait()
-    to_right.wait()
-    to_left.wait()
-    to_mirror.wait()
+
+    @pl.when(has_right)
+    def _():
+        to_right.wait_send()
+        to_left.wait_recv()
+
+    @pl.when(has_left)
+    def _():
+        to_left.wait_send()
+        to_right.wait_recv()
+
     own = previous[...]
-    has_left = jnp.where(plane > 0, 1.0, 0.0).astype(jnp.float32)
-    has_right = jnp.where(plane < planes - 1, 1.0, 0.0).astype(jnp.float32)
     span = lengths.shape[1]
     offline = (
-        coupling[0] * (from_left[...] * has_left)
-        + coupling[1] * (from_right[...] * has_right)
+        coupling[0] * from_left[...]
+        + coupling[1] * from_right[...]
         + coupling[2] * pltpu.roll(own, 1, 1)
         + coupling[3] * pltpu.roll(own, span - 1, 1)
     )
@@ -280,23 +318,27 @@
     levels = lax.rem(lax.broadcasted_iota(jnp.int32, (rows, span), 0), depth) + base
     active = jnp.where(levels < lengths, 1.0, 0.0).astype(jnp.float32)
     source[...] = (residual[...] + offline) * active
-    chosen = jnp.where(
-        lax.broadcasted_iota(jnp.int32, (span, span), 0) == partner_map[...], 1.0, 0.0
-    ).astype(jnp.float32)
-    partner = jnp.dot(
-        facing[...], chosen, precision=lax.Precision.HIGHEST, preferred_element_type=jnp.float32
-    )
-    first_rows = first.reshape(extent * extent * middle, span)
-    wake = total(
-        [
-            first_rows[pl.ds(inner * middle, extent, stride=extent * middle), :]
-            * spread(partner, inner, extent)
-            for inner in range(extent)
-        ]
-    )
-    weight = flag[...].astype(jnp.float32) * jnp.where(wall == 0, 1.0, 0.0).astype(jnp.float32)
-    bottom_rows = pl.ds(0, extent, stride=depth)
-    source[bottom_rows, :] = source[bottom_rows, :] - wake * weight * mask_at(base)
+    @pl.when(wall == 0)
+    def _():
+        first_fetch.wait()
+        to_mirror.wait()
+        chosen = jnp.where(
+            lax.broadcasted_iota(jnp.int32, (span, span), 0) == partner_map[...], 1.0, 0.0
+        ).astype(jnp.float32)
+        partner = jnp.dot(
+            facing[...], chosen, precision=lax.Precision.HIGHEST, preferred_element_type=jnp.float32
+        )
+        first_rows = first.reshape(extent * extent * middle, span)
+        wake = total(
+            [
+                first_rows[pl.ds(inner * middle, extent, stride=extent * middle), :]
+                * spread(partner, inner, extent)
+                for inner in range(extent)
+            ]
+        )
+        weight = flag[...].astype(jnp.float32)
+        bottom_rows = pl.ds(0, extent, stride=depth)
+        source[bottom_rows, :] = source[bottom_rows, :] - wake * weight * mask_at(base)
 
     def source_at(step):
         return source[pl.ds(level_at(step), extent, stride=depth), :]
@@ -443,7 +485,7 @@
 
     result = pl.pallas_call(
         functools.partial(kernel, extent, depth),
-        out_shape=jax.ShapeDtypeStruct((extent * depth, span), f32),
+        out_shape=pltpu.VMEM((extent * depth, span), f32),
         in_specs=[pl.BlockSpec(memory_space=pl.ANY)] * 7,
         out_specs=whole,
         scratch_shapes=[

time: 20.3 us -> 16.2 us (0.80)
  Pallas kernels: 18.5 us -> 15.4 us
  local copies, waits for them, and re-layouts: 1.57 us -> 0.66 us
    pallas_call x1, Pallas kernels: 18.5 us -> 15.4 us  [per_device(): pl.pallas_call(functools.partial(kernel, extent, depth), out_shape=pltpu....]
    unnamed x1, local copies, waits for them, and re-layouts: 1.57 us -> 0.66 us
where the time goes in v4:
time: 16.2 us; the launch traced here: 16.1 us
  Pallas kernels  15.4 us (95%)
  local copies, waits for them, and re-layouts  0.66 us (4%)
    pallas_call x1, Pallas kernels, per_device(): pl.pallas_call(functools.partial(kernel, extent, depth), out_shape=pltpu....  15.4 us
    unnamed x1, local copies, waits for them, and re-layouts  0.66 us

profile of v4, /device:TPU:0, one launch (start us, length us, event | category | flops | bytes accessed | tf_op | source)
XLA Modules:
  0.0 16.1 jit_solution(9465356990562131203)
XLA Ops:
  0.0 15.4 %shard_map.73 = f32[256,128]{1,0:T(8,128)S(1)} custom-call(f32[3,256,16,128]{3,2,1,0:T(8,128)} %bitcast.8, f32[256,128]{1,0:T(8,128)} %bitcast.10, f32[256,128]{1,0:T(8,128)} %bitcast.11, f32[4,256,128]{2,1,0:T(8,128)} %bitcast.9, s32[1,128]{1,0:T(1,128)} %partner_far.1, s32[1,128]{1,0:T(1,128)} %length_far.1, s32[1,128]{1,0:T(1,128)} %flag_far.1), custom_call_target="tpu_custom_call" | custom-call | tf_op jit(solution)/shard_map/pallas_call | solution.py:486
  15.4 0.7 %copy.10 = f32[16,16,1,128]{3,2,1,0:T(1,128)} copy(f32[16,16,1,128]{3,2,1,0:T(1,128)S(1)} %bitcast.7) | data formatting | bytes 262144

commit v5 on v4

--- a/solution.py
+++ b/solution.py
@@ -228,8 +228,11 @@
         return block * mask + jnp.where(place == row, 1.0 - mask, 0.0)
 
     fetches[2].wait()
-    for row in range(extent):
-        schur[pl.ds(row * extent, extent), :] = diagonal(0, row)
+    started = [diagonal(0, row) for row in range(extent)]
+    state = (
+        tuple(block[:half] for block in started[:half]),
+        tuple(block[half:] for block in started),
+    )
     fetches[3].wait()
     fetches[4].start()
     fetches[5].start()
@@ -239,7 +242,14 @@
     fetches[0].wait()
     bottom[...] = previous[pl.ds(0, extent, stride=depth), :]
 
-    def advance(step, _):
+    def keep_state(store, state):
+        for row in range(half):
+            store[row * half : (row + 1) * half, :] = state[0][row]
+        for row in range(extent):
+            here = (half + row) * half
+            store[here : here + half, :] = state[1][row]
+
+    def advance(step, state):
         @pl.when(step == 3)
         def _():
             pl.semaphore_wait(barrier, greetings)
@@ -255,20 +265,19 @@
         level = level_at(step)
         start = pl.multiple_of(step * (extent * extent), extent * extent)
         mask = mask_at(level + base + 1 - wall)
-        low, high, beyond = [], [], []
-        next_low, next_high = [], []
+        low, high = list(state[0]) + [None] * half, list(state[1])
+        beyond, next_low, next_high = [], [], []
+        keep_state(schur, state)
         following = jnp.minimum(step + 1, depth - 1)
         kept = jnp.where(step < depth - 1, 1.0, 0.0).astype(jnp.float32)
         for row in range(extent):
-            low.append(schur[pl.ds(start + row * extent, half), :] if row < half else None)
-            high.append(schur[pl.ds(start + row * extent + half, half), :])
             block = near[pl.ds(row * extent * depth + level, extent, stride=depth), :] * mask
             beyond.append((block[:half], block[half:]))
             block = diagonal(following, row) * kept
-            next_low.append(block[:half])
+            if row < half:
+                next_low.append(block[:half])
             next_high.append(block[half:])
         scales = factor(low, high, beyond, (next_low, next_high))
-        ahead = pl.multiple_of((step + 1) * (extent * extent), extent * extent)
         scale_at = pl.multiple_of(step * extent, extent)
         scale[pl.ds(scale_at, half), :] = scales[0]
         scale[pl.ds(scale_at + half, half), :] = scales[1]
@@ -278,18 +287,9 @@
                 inverse[pl.ds(start + row * extent + half, half), :] = high[row]
             carry[pl.ds(start + row * extent, half), :] = beyond[row][0]
             carry[pl.ds(start + row * extent + half, half), :] = beyond[row][1]
-            if row < half:
-                schur[pl.ds(ahead + row * extent, half), :] = next_low[row]
-            schur[pl.ds(ahead + row * extent + half, half), :] = next_high[row]
-        return 0
-
-    lax.fori_loop(0, depth, advance, 0)
-    done = depth * extent * extent
-    upper = half * extent
-    block_out[0:upper, :] = schur[done : done + upper, :]
-    for row in range(half):
-        here = done + (half + row) * extent + half
-        block_out[upper + row * half : upper + (row + 1) * half, :] = schur[here : here + half, :]
+        return tuple(next_low), tuple(next_high)
+
+    keep_state(block_out, lax.fori_loop(0, depth, advance, state, unroll=2))
     to_across = send(block_out, block_in, 3, across)
     to_across.start()
 
@@ -411,19 +411,9 @@
 
     to_across.wait()
     last = (depth - 1) * extent * extent
-    low, high = [], []
-    for row in range(extent):
-        here = last + row * extent
-        if row < half:
-            low.append(schur[here : here + half, :] + block_in[row * extent : row * extent + half, :])
-            high.append(
-                schur[here + half : here + extent, :]
-                + block_in[row * extent + half : (row + 1) * extent, :]
-            )
-        else:
-            low.append(None)
-            at = upper + (row - half) * half
-            high.append(schur[here + half : here + extent, :] + block_in[at : at + half, :])
+    met = schur[...] + block_in[...]
+    low = [met[row * half : (row + 1) * half] for row in range(half)] + [None] * half
+    high = [met[(half + row) * half : (half + row + 1) * half] for row in range(extent)]
     scales = factor(low, high, None, None)
     for row in range(extent):
         inverse[last + row * extent : last + row * extent + half, :] = low[row]
@@ -498,7 +488,7 @@
             pltpu.VMEM((block, depth, span), f32),
             pltpu.VMEM((block, depth, span), f32),
             pltpu.VMEM((block, depth // 2, span), f32),
-            room(block * (depth + 1)),
+            room(block * 3 // 4),
             room(block * depth),
             room(block * depth),
             room(extent * depth),

time: 16.2 us -> 16 us (0.988)
  Pallas kernels: 15.4 us -> 15.2 us
    pallas_call x1, Pallas kernels: 15.4 us -> 15.2 us  [per_device(): pl.pallas_call(functools.partial(kernel, extent, depth), out_shape=pltpu....]
where the time goes in v5:
time: 16 us; the launch traced here: 15.9 us
  Pallas kernels  15.2 us (95%)
  local copies, waits for them, and re-layouts  0.66 us (4%)
    pallas_call x1, Pallas kernels, per_device(): pl.pallas_call(functools.partial(kernel, extent, depth), out_shape=pltpu....  15.2 us
    unnamed x1, local copies, waits for them, and re-layouts  0.66 us

profile of v5, /device:TPU:0, one launch (start us, length us, event | category | flops | bytes accessed | tf_op | source)
XLA Modules:
  0.0 15.9 jit_solution(18261683293603896802)
XLA Ops:
  0.0 15.2 %shard_map.73 = f32[256,128]{1,0:T(8,128)S(1)} custom-call(f32[3,256,16,128]{3,2,1,0:T(8,128)} %bitcast.8, f32[256,128]{1,0:T(8,128)} %bitcast.10, f32[256,128]{1,0:T(8,128)} %bitcast.11, f32[4,256,128]{2,1,0:T(8,128)} %bitcast.9, s32[1,128]{1,0:T(1,128)} %partner_far.1, s32[1,128]{1,0:T(1,128)} %length_far.1, s32[1,128]{1,0:T(1,128)} %flag_far.1), custom_call_target="tpu_custom_call" | custom-call | tf_op jit(solution)/shard_map/pallas_call | solution.py:476
  15.2 0.7 %copy.10 = f32[16,16,1,128]{3,2,1,0:T(1,128)} copy(f32[16,16,1,128]{3,2,1,0:T(1,128)S(1)} %bitcast.7) | data formatting | bytes 262144

commit v6 on v5

--- a/solution.py
+++ b/solution.py
@@ -289,7 +289,17 @@
             carry[pl.ds(start + row * extent + half, half), :] = beyond[row][1]
         return tuple(next_low), tuple(next_high)
 
-    keep_state(block_out, lax.fori_loop(0, depth, advance, state, unroll=2))
+    change_low, change_high = lax.fori_loop(0, depth, advance, state, unroll=2)
+    small = lax.broadcasted_iota(jnp.int32, change_low[0].shape, 0)
+    ends = change_high[half]
+    for row in range(half):
+        lower_right = change_high[half + row]
+        block_out[row * half : (row + 1) * half, :] = jnp.where(
+            small >= row, change_low[row], lower_right
+        )
+        block_out[(half + row) * half : (half + row + 1) * half, :] = change_high[row]
+        ends = jnp.where(small == row, lower_right, ends)
+    block_out[extent * half : (extent + 1) * half, :] = ends
     to_across = send(block_out, block_in, 3, across)
     to_across.start()
 
@@ -405,15 +415,24 @@
         following = halves_of(source_at(jnp.minimum(step + 1, depth - 1)))
         return tuple(given - less for given, less in zip(following, change))
 
-    lax.fori_loop(0, depth, forward, halves_of(source_at(0)))
+    lax.fori_loop(0, depth, forward, halves_of(source_at(0)), unroll=4)
     vector_across = send(vector_out, vector_in, 4, across)
     vector_across.start()
 
     to_across.wait()
     last = (depth - 1) * extent * extent
-    met = schur[...] + block_in[...]
-    low = [met[row * half : (row + 1) * half] for row in range(half)] + [None] * half
-    high = [met[(half + row) * half : (half + row + 1) * half] for row in range(extent)]
+    ends = block_in[extent * half : (extent + 1) * half, :]
+    low, high = [], []
+    for row in range(extent):
+        at = row * half
+        low.append(schur[at : at + half, :] + block_in[at : at + half, :] if row < half else None)
+        if row < half:
+            here = (half + row) * half
+            high.append(schur[here : here + half, :] + block_in[here : here + half, :])
+        else:
+            here = (half + row) * half
+            column = block_in[pl.ds(row - half, half, stride=half), :]
+            high.append(schur[here : here + half, :] + jnp.where(small == row - half, ends, column))
     scales = factor(low, high, None, None)
     for row in range(extent):
         inverse[last + row * extent : last + row * extent + half, :] = low[row]
@@ -459,7 +478,7 @@
         put(step, value)
         return tuple(value)
 
-    lax.fori_loop(0, depth - 1, backward, tuple(value))
+    lax.fori_loop(0, depth - 1, backward, tuple(value), unroll=5)
 
 
 def per_device(
@@ -499,8 +518,8 @@
             room(extent),
             room(extent * depth),
             room(extent * depth),
-            room(block * 3 // 4),
-            room(block * 3 // 4),
+            room((extent + 1) * extent // 2),
+            room((extent + 1) * extent // 2),
             room(extent),
             room(extent),
             pltpu.SemaphoreType.DMA((11,)),

time: 16 us -> 15.4 us (0.963)
  Pallas kernels: 15.2 us -> 14.5 us
    pallas_call x1, Pallas kernels: 15.2 us -> 14.5 us  [per_device(): pl.pallas_call(functools.partial(kernel, extent, depth), out_shape=pltpu....]
where the time goes in v6:
time: 15.4 us; the launch traced here: 15.2 us
  Pallas kernels  14.5 us (94%)
  local copies, waits for them, and re-layouts  0.66 us (4%)
    pallas_call x1, Pallas kernels, per_device(): pl.pallas_call(functools.partial(kernel, extent, depth), out_shape=pltpu....  14.5 us
    unnamed x1, local copies, waits for them, and re-layouts  0.66 us

profile of v6, /device:TPU:0, one launch (start us, length us, event | category | flops | bytes accessed | tf_op | source)
XLA Modules:
  0.0 15.2 jit_solution(1283013419343731856)
XLA Ops:
  0.0 14.5 %shard_map.73 = f32[256,128]{1,0:T(8,128)S(1)} custom-call(f32[3,256,16,128]{3,2,1,0:T(8,128)} %bitcast.8, f32[256,128]{1,0:T(8,128)} %bitcast.10, f32[256,128]{1,0:T(8,128)} %bitcast.11, f32[4,256,128]{2,1,0:T(8,128)} %bitcast.9, s32[1,128]{1,0:T(1,128)} %partner_far.1, s32[1,128]{1,0:T(1,128)} %length_far.1, s32[1,128]{1,0:T(1,128)} %flag_far.1), custom_call_target="tpu_custom_call" | custom-call | tf_op jit(solution)/shard_map/pallas_call | solution.py:495
  14.5 0.7 %copy.10 = f32[16,16,1,128]{3,2,1,0:T(1,128)} copy(f32[16,16,1,128]{3,2,1,0:T(1,128)S(1)} %bitcast.7) | data formatting | bytes 262144

commit v7 on v6

--- a/solution.py
+++ b/solution.py
@@ -14,7 +14,7 @@
     return jnp.broadcast_to(row[index : index + 1, :], (rows, row.shape[1]))
 
 
-def factor(low, high, right, following):
+def factor(low, high, right, following, plain_rows):
     extent = len(high)
     half = high[0].shape[0]
     group = 4
@@ -46,7 +46,10 @@
             high[pivot] = jnp.where(place < at, pivot_high, jnp.where(here, 1.0, 0.0))
         if right is not None:
             scaled_right = tuple(part * inverse for part in right[pivot])
-            finished.append((right[pivot], scaled_right))
+            finished.append((pivot * extent, scaled_right))
+            for part in range(2):
+                at_part = pivot * extent + part * half
+                plain_rows[at_part : at_part + half, :] = right[pivot][part]
             right[pivot] = scaled_right
         for row in range(pivot + 1, extent):
             by = spread(pivot_low if row < half else pivot_high, row % half, half)
@@ -66,7 +69,10 @@
         if len(finished) == group:
             next_low, next_high = following
             for row in range(extent):
-                bys = [spread(plain[row // half], row % half, half) for plain, _ in finished]
+                bys = [
+                    jnp.broadcast_to(plain_rows[start + row : start + row + 1, :], place.shape)
+                    for start, _ in finished
+                ]
                 if row < half:
                     next_low[row] = next_low[row] - total(
                         [by * scaled[0] for by, (_, scaled) in zip(bys, finished)]
@@ -115,6 +121,7 @@
     reduced,
     fixed,
     scale,
+    plain_rows,
     bottom,
     facing,
     from_left,
@@ -277,7 +284,7 @@
             if row < half:
                 next_low.append(block[:half])
             next_high.append(block[half:])
-        scales = factor(low, high, beyond, (next_low, next_high))
+        scales = factor(low, high, beyond, (next_low, next_high), plain_rows)
         scale_at = pl.multiple_of(step * extent, extent)
         scale[pl.ds(scale_at, half), :] = scales[0]
         scale[pl.ds(scale_at + half, half), :] = scales[1]
@@ -433,7 +440,7 @@
             here = (half + row) * half
             column = block_in[pl.ds(row - half, half, stride=half), :]
             high.append(schur[here : here + half, :] + jnp.where(small == row - half, ends, column))
-    scales = factor(low, high, None, None)
+    scales = factor(low, high, None, None, None)
     for row in range(extent):
         inverse[last + row * extent : last + row * extent + half, :] = low[row]
         if row >= half:
@@ -514,6 +521,7 @@
             room(extent * depth),
             room(extent * depth),
             room(extent * depth),
+            room(block),
             room(extent),
             room(extent),
             room(extent * depth),

time: 15.4 us -> 15.2 us (0.987)
  no operation moved by 1% of the time
where the time goes in v7:
time: 15.2 us; the launch traced here: 15.1 us
  Pallas kernels  14.4 us (95%)
  local copies, waits for them, and re-layouts  0.66 us (4%)
    pallas_call x1, Pallas kernels, per_device(): pl.pallas_call(functools.partial(kernel, extent, depth), out_shape=pltpu....  14.4 us
    unnamed x1, local copies, waits for them, and re-layouts  0.66 us

profile of v7, /device:TPU:0, one launch (start us, length us, event | category | flops | bytes accessed | tf_op | source)
XLA Modules:
  0.0 15.1 jit_solution(4538711008983795373)
XLA Ops:
  0.0 14.4 %shard_map.73 = f32[256,128]{1,0:T(8,128)S(1)} custom-call(f32[3,256,16,128]{3,2,1,0:T(8,128)} %bitcast.8, f32[256,128]{1,0:T(8,128)} %bitcast.10, f32[256,128]{1,0:T(8,128)} %bitcast.11, f32[4,256,128]{2,1,0:T(8,128)} %bitcast.9, s32[1,128]{1,0:T(1,128)} %partner_far.1, s32[1,128]{1,0:T(1,128)} %length_far.1, s32[1,128]{1,0:T(1,128)} %flag_far.1), custom_call_target="tpu_custom_call" | custom-call | tf_op jit(solution)/shard_map/pallas_call | solution.py:502
  14.4 0.7 %copy.10 = f32[16,16,1,128]{3,2,1,0:T(1,128)} copy(f32[16,16,1,128]{3,2,1,0:T(1,128)S(1)} %bitcast.7) | data formatting | bytes 262144

commit v8 on v7

--- a/solution.py
+++ b/solution.py
@@ -296,7 +296,7 @@
             carry[pl.ds(start + row * extent + half, half), :] = beyond[row][1]
         return tuple(next_low), tuple(next_high)
 
-    change_low, change_high = lax.fori_loop(0, depth, advance, state, unroll=2)
+    change_low, change_high = lax.fori_loop(0, depth, advance, state, unroll=4)
     small = lax.broadcasted_iota(jnp.int32, change_low[0].shape, 0)
     ends = change_high[half]
     for row in range(half):

time: 15.2 us -> 15 us (0.987)
  Pallas kernels: 14.4 us -> 14.2 us
    pallas_call x1, Pallas kernels: 14.4 us -> 14.2 us  [per_device(): pl.pallas_call(functools.partial(kernel, extent, depth), out_shape=pltpu....]
where the time goes in v8:
time: 15 us; the launch traced here: 14.9 us
  Pallas kernels  14.2 us (95%)
  local copies, waits for them, and re-layouts  0.66 us (4%)
    pallas_call x1, Pallas kernels, per_device(): pl.pallas_call(functools.partial(kernel, extent, depth), out_shape=pltpu....  14.2 us
    unnamed x1, local copies, waits for them, and re-layouts  0.66 us

profile of v8, /device:TPU:0, one launch (start us, length us, event | category | flops | bytes accessed | tf_op | source)
XLA Modules:
  0.0 14.9 jit_solution(18336953564486102718)
XLA Ops:
  0.0 14.2 %shard_map.73 = f32[256,128]{1,0:T(8,128)S(1)} custom-call(f32[3,256,16,128]{3,2,1,0:T(8,128)} %bitcast.8, f32[256,128]{1,0:T(8,128)} %bitcast.10, f32[256,128]{1,0:T(8,128)} %bitcast.11, f32[4,256,128]{2,1,0:T(8,128)} %bitcast.9, s32[1,128]{1,0:T(1,128)} %partner_far.1, s32[1,128]{1,0:T(1,128)} %length_far.1, s32[1,128]{1,0:T(1,128)} %flag_far.1), custom_call_target="tpu_custom_call" | custom-call | tf_op jit(solution)/shard_map/pallas_call | solution.py:502
  14.2 0.7 %copy.10 = f32[16,16,1,128]{3,2,1,0:T(1,128)} copy(f32[16,16,1,128]{3,2,1,0:T(1,128)S(1)} %bitcast.7) | data formatting | bytes 262144
